TPU v7x, 128 devices: a whole 4x4x4 slice. The times are simulated.
128 devices in a mesh: gz: 8 (over y, core), ta: 16 (over x, z).
Axes of the slice: x: 4, y: 4, z: 4, core: 2. Of those that a mesh axis runs over, the one named last changes fastest.
Arguments:
- basis: bfloat16 [2048, 128, 3072], P(('gz', 'ta')), may hold values from -0.078125 to 0.078125
- sources: bfloat16 [2048, 24, 3072], P(('gz', 'ta')), may hold values from -2000 to 2000
- old_coeffs: bfloat16 [32768, 3200], P(('gz', 'ta')), may hold values from -0.01171875 to 0.01171875
- eigenvalues: float32 [400], replicated, may hold values from 0.00239208 to 0.023920799
- dest_owner: int32 [32768], P(('gz', 'ta')), may hold values from 0 to 127, as said below
- new_pos: int32 [32768], P(('gz', 'ta')), may hold values from 0 to 255, as said below
Outputs:
- guesses: float32 [2048, 24, 3072], P(('gz', 'ta'))
- correlations: float32 [400, 24], replicated
Inputs may be any that keep to these rules, and one draw needn't show every extreme that they name: `dest_owner`: on every device no owner is named by more than 4 records and some owner by exactly 4; over all devices every owner is named by exactly 256 records. `new_pos`: the records naming one owner carry distinct rows.
All inputs are finite; a program needn't handle non-finite values.
Results may differ from a plain program's by a relative error of at most 0.007.
Values may be sent and summed in bfloat16 or wider, within the bound.
A program may use at most 64 MiB of HBM per device.

v0:
```python
import jax
import jax.numpy as jnp
from jax import lax
from jax.sharding import PartitionSpec as P


def shards(basis, sources, old_coeffs, eigenvalues, dest_owner, new_pos):
    along_z = lax.axis_size("gz")
    along_t = lax.axis_size("ta")
    device_count = along_z * along_t
    records = old_coeffs.shape[0]
    capacity = 2 * records // device_count
    record_width = old_coeffs.shape[1]
    block_count = basis.shape[0]
    half_rows = basis.shape[1] // 2
    source_count = sources.shape[1] // 2
    mode_count = eigenvalues.shape[0]
    local_squares = jnp.sum(jnp.square(sources.astype(jnp.float32)), axis=(0, 2))
    square_sum = lax.psum(local_squares, ("gz", "ta"))
    owners = lax.broadcasted_iota(jnp.int32, (records, device_count), 1)
    onehot = (dest_owner[:, None] == owners).astype(jnp.int32)
    earlier = jnp.cumsum(onehot, axis=0) - onehot
    slot_rank = jnp.sum(earlier * onehot, axis=1)
    targets = dest_owner * capacity + slot_rank
    outgoing = (
        jnp.zeros((device_count * capacity, record_width), old_coeffs.dtype)
        .at[targets]
        .set(old_coeffs)
    )
    positions = jnp.full((device_count * capacity,), records, jnp.int32).at[targets].set(new_pos)
    arrived, arrived_rows = (
        lax.all_to_all(
            outgoing.reshape(device_count, capacity, record_width),
            ("gz", "ta"),
            split_axis=0,
            concat_axis=0,
            tiled=True,
        ),
        lax.all_to_all(
            positions.reshape(device_count, capacity),
            ("gz", "ta"),
            split_axis=0,
            concat_axis=0,
            tiled=True,
        ),
    )
    coeff_table = (
        jnp.zeros((records, record_width), old_coeffs.dtype)
        .at[arrived_rows.reshape(-1)]
        .set(arrived.reshape(-1, record_width), mode="drop")
    )
    coeffs = coeff_table.reshape(block_count, mode_count, 2 * half_rows)
    products = jnp.einsum("bkj,bsj->bks", basis, sources, preferred_element_type=jnp.float32)
    real_half = (
        products[:, :half_rows, :source_count] + products[:, half_rows:, source_count:]
    ).astype(jnp.bfloat16)
    imag_half = (
        products[:, :half_rows, source_count:] - products[:, half_rows:, :source_count]
    ).astype(jnp.bfloat16)
    stacked = jnp.concatenate(
        [jnp.concatenate([real_half, imag_half], 2), jnp.concatenate([imag_half, -real_half], 2)], 1
    )
    partial_correlation = jnp.einsum(
        "bmk,bks->ms", coeffs, stacked, preferred_element_type=jnp.float32
    )
    proj = lax.psum(partial_correlation, ("gz", "ta"))
    norm_sq = square_sum[:source_count] + square_sum[source_count:]
    total_cells = 2 * block_count * device_count * basis.shape[2]
    scale = jnp.sqrt(jnp.float32(total_cells)) * lax.rsqrt(norm_sq + 1e-06)
    correlations = proj * jnp.concatenate([scale, scale])[None, :]
    weights = (correlations / eigenvalues[:, None]).astype(jnp.bfloat16)
    mixed = jnp.einsum("bmk,ms->bks", coeffs, weights, preferred_element_type=jnp.float32)
    real_coef = jnp.swapaxes(
        (mixed[:, :half_rows, :source_count] - mixed[:, half_rows:, source_count:]).astype(
            jnp.bfloat16
        ),
        1,
        2,
    )
    imag_coef = jnp.swapaxes(
        (mixed[:, :half_rows, source_count:] + mixed[:, half_rows:, :source_count]).astype(
            jnp.bfloat16
        ),
        1,
        2,
    )
    combined = jnp.concatenate(
        [jnp.concatenate([real_coef, -imag_coef], 2), jnp.concatenate([imag_coef, real_coef], 2)], 1
    )
    guesses = jnp.einsum("bsk,bkj->bsj", combined, basis, preferred_element_type=jnp.float32)
    return (guesses, correlations)


def solution(mesh):
    in_specs = (
        P(("gz", "ta"), None, None),
        P(("gz", "ta"), None, None),
        P(("gz", "ta"), None),
        P(),
        P(("gz", "ta")),
        P(("gz", "ta")),
    )
    out_specs = (P(("gz", "ta"), None, None), P())
    return jax.shard_map(shards, mesh=mesh, in_specs=in_specs, out_specs=out_specs, check_vma=False)
```

profile of v0, /device:TPU:0, one launch (start us, length us, event | category | flops | bytes accessed | tf_op | source)
XLA Modules:
  0.0 161.5 jit_solution(6998010093737762058)
XLA Ops:
  0.6 0.8 copy.10
  1.4 0.2 fusion.4
  1.7 0.9 fusion.10
  2.6 0.7 compare_select_fusion.1
  3.3 1.6 scatter_custom_fusion
  4.8 0.7 all_to_all.9
  5.6 11.1 %all-to-all-start = ((s32[128,1,4]{2,1,0:T(1,128)}), s32[128,1,4]{2,1,0:T(1,128)S(1)}, u32[]{:S(2)}, u32[]{:S(2)}) async-start(s32[128,1,4]{2,1,0:T(1,128)} %bitcast.4), calls=%async_computation | async-start | bytes 131072 | tf_op jit(solution)/shard_map/all_to_all | solution.py:39
  16.7 4.9 %scatter_custom_fusion.1 = bf16[512,3200]{1,0:T(8,128)(2,1)S(1)} fusion(s32[256]{0:T(256)S(1)} %compare_select_fusion.1, bf16[256,3200]{1,0:T(8,128)(2,1)} %param.8, bf16[]{:T(256)} %constant.8.clone.1), kind=kCustom, calls=%fused_computation.4 | custom fusion | bytes 3277312 | tf_op jit(solution)/shard_map/scatter | solution.py:28
  21.6 2.4 %reshape.67 = bf16[128,4,3200]{2,1,0:T(4,128)(2,1)} reshape(bf16[512,3200]{1,0:T(8,128)(2,1)S(1)} %scatter_custom_fusion.1) | data formatting | bytes 6553600 | tf_op jit(solution)/shard_map/reshape | solution.py:33
  24.0 2.2 %all-to-all-done = s32[128,1,4]{2,1,0:T(1,128)S(1)} async-done(((s32[128,1,4]{2,1,0:T(1,128)}), s32[128,1,4]{2,1,0:T(1,128)S(1)}, u32[]{:S(2)}, u32[]{:S(2)}) %all-to-all-start) | async-done | bytes 2080 | tf_op jit(solution)/shard_map/all_to_all | solution.py:39
  26.2 0.6 copy-done
  26.8 7.8 %all-to-all-start.1 = ((bf16[128,4,3200]{2,1,0:T(4,128)(2,1)}), bf16[128,4,3200]{2,1,0:T(4,128)(2,1)S(1)}, u32[]{:S(2)}, u32[]{:S(2)}) async-start(bf16[128,4,3200]{2,1,0:T(4,128)(2,1)} %reshape.67), calls=%async_computation.1 | async-start | bytes 6553600 | tf_op jit(solution)/shard_map/all_to_all | solution.py:32
  34.6 8.6 %fusion.40 = f32[16,128,24]{1,2,0:T(8,128)S(1)} fusion(bf16[16,128,3072]{2,1,0:T(8,128)(2,1)} %param.6, bf16[16,24,3072]{2,1,0:T(8,128)(2,1)} %param.7), kind=kOutput, calls=%fused_computation.58 | convolution fusion | flops 301989888 | bytes 15138816 | tf_op jit(solution)/shard_map/bkj,bsj->bks/dot_general | solution.py:53
  43.2 0.1 fusion.7
  43.3 0.7 fusion.38
  44.1 2.2 %multiply_reduce_fusion = f32[24]{0:T(128)S(1)} fusion(bf16[16,24,3072]{2,1,0:T(8,128)(2,1)} %param.7), kind=kLoop, calls=%fused_computation.3 | loop fusion | flops 3538920 | bytes 2359392 | tf_op jit(solution)/shard_map/reduce_sum | solution.py:18
  46.3 0.5 broadcast.64
  46.8 1.6 %reduce.3 = s32[128,4]{1,0:T(8,128)S(1)} reduce(s32[128,1,4]{2,1,0:T(1,128)} %copy-done, s32[]{:T(128)} %broadcast.64), dimensions={1}, to_apply=%all_to_all.10.reduce_sub_computation.3 | reduce | bytes 4100 | tf_op jit(solution)/shard_map/all_to_all | solution.py:39
  48.5 0.1 reshape.66
  48.6 27.9 %all-to-all-done.1 = bf16[128,4,3200]{2,1,0:T(4,128)(2,1)S(1)} async-done(((bf16[128,4,3200]{2,1,0:T(4,128)(2,1)}), bf16[128,4,3200]{2,1,0:T(4,128)(2,1)S(1)}, u32[]{:S(2)}, u32[]{:S(2)}) %all-to-all-start.1) | async-done | bytes 3276832 | tf_op jit(solution)/shard_map/all_to_all | solution.py:32
  76.5 2.4 %reshape.90 = bf16[512,3200]{1,0:T(8,128)(2,1)} reshape(bf16[128,4,3200]{2,1,0:T(4,128)(2,1)S(1)} %all-to-all-done.1) | data formatting | bytes 6553600 | tf_op jit(solution)/shard_map/reshape | solution.py:50
  78.9 6.7 %scatter_custom_fusion.2 = bf16[256,3200]{1,0:T(8,128)(2,1)S(1)} fusion(s32[512]{0:T(512)S(1)} %bitcast.35, bf16[512,3200]{1,0:T(8,128)(2,1)} %reshape.90, bf16[]{:T(256)} %constant.8.clone.1), kind=kCustom, calls=%fused_computation.7 | custom fusion | bytes 1638912 | tf_op jit(solution)/shard_map/scatter | solution.py:50
  85.7 2.0 %reshape.69 = bf16[16,400,128]{2,1,0:T(8,128)(2,1)S(1)} reshape(bf16[256,3200]{1,0:T(8,128)(2,1)S(1)} %scatter_custom_fusion.2) | data formatting | bytes 3276800 | tf_op jit(solution)/shard_map/reshape | solution.py:52
  87.7 0.6 convolution_bitcast_fusion
  88.2 63.9 %all-reduce = (f32[400,24]{0,1:T(8,128)S(1)}, f32[24]{0:T(128)S(1)}) all-reduce(f32[400,24]{0,1:T(8,128)S(1)} %convolution_bitcast_fusion, f32[24]{0:T(128)S(1)} %multiply_reduce_fusion), channel_id=1, replica_groups=mesh['gz'=8,'ta'=16] {'gz','ta'}, use_global_device_ids=true, to_apply=%region_6.7 | all-reduce | flops 9624 | bytes 76992 | tf_op jit(solution)/shard_map/psum | solution.py:66
  152.1 0.1 rsqrt_multiply_fusion
  152.2 0.1 pad_maximum_fusion
  152.3 0.1 broadcast_multiply_fusion
  152.4 0.3 fusion.30
  152.7 0.1 fusion.36
  152.8 0.1 fusion.27
  152.9 8.6 %fusion.19 = f32[16,24,3072]{2,1,0:T(8,128)} fusion(bf16[16,128,3072]{2,1,0:T(8,128)(2,1)} %param.6, bf16[16,12,64]{2,1,0:T(8,128)(2,1)S(1)} %fusion.27, bf16[16,12,64]{2,1,0:T(8,128)(2,1)S(1)} %get-tuple-element.5, bf16[16,12,64]{2,1,0:T(8,128)(2,1)S(1)} %get-tuple-element.4), kind=kOutput, calls=%fused_computation.31 | convolution fusion | flops 302383104 | bytes 17375232 | tf_op jit(solution)/shard_map/bsk,bkj->bsj/dot_general | solution.py:90
  (16 shorter events, 0.1 us)
Async XLA Ops:
  5.6 20.6 %all-to-all-start = ((s32[128,1,4]{2,1,0:T(1,128)}), s32[128,1,4]{2,1,0:T(1,128)S(1)}, u32[]{:S(2)}, u32[]{:S(2)}) async-start(s32[128,1,4]{2,1,0:T(1,128)} %bitcast.4), calls=%async_computation | async-start | bytes 131072 | tf_op jit(solution)/shard_map/all_to_all | solution.py:39
  26.2 0.6 copy-start
  26.8 49.7 %all-to-all-start.1 = ((bf16[128,4,3200]{2,1,0:T(4,128)(2,1)}), bf16[128,4,3200]{2,1,0:T(4,128)(2,1)S(1)}, u32[]{:S(2)}, u32[]{:S(2)}) async-start(bf16[128,4,3200]{2,1,0:T(4,128)(2,1)} %reshape.67), calls=%async_computation.1 | async-start | bytes 6553600 | tf_op jit(solution)/shard_map/all_to_all | solution.py:32
  78.9 8.7 %copy-start.1 = (bf16[16,64,12]{1,2,0:T(8,128)(2,1)S(1)}, bf16[16,64,12]{1,2,0:T(8,128)(2,1)}, u32[]{:S(2)}) copy-start(bf16[16,64,12]{1,2,0:T(8,128)(2,1)} %get-tuple-element.6) | copy-start | bytes 73732
  78.9 8.7 %copy-start.2 = (bf16[16,64,12]{1,2,0:T(8,128)(2,1)S(1)}, bf16[16,64,12]{1,2,0:T(8,128)(2,1)}, u32[]{:S(2)}) copy-start(bf16[16,64,12]{1,2,0:T(8,128)(2,1)} %get-tuple-element.7) | copy-start | bytes 73732
  78.9 73.4 %copy-start.4 = (f32[400]{0:T(512)S(1)}, f32[400]{0:T(512)}, u32[]{:S(2)}) copy-start(f32[400]{0:T(512)} %param.9) | copy-start | bytes 4804
  152.4 9.1 %copy-start.3 = (f32[400,24]{0,1:T(8,128)}, f32[400,24]{0,1:T(8,128)S(1)}, u32[]{:S(2)}) copy-start(f32[400,24]{0,1:T(8,128)S(1)} %broadcast_multiply_fusion) | copy-start | bytes 115204
where the time goes:
time: 163 us; the launch traced here: 162 us
  blocking collectives  63.9 us (39%)
  waiting for transfers between devices  30.1 us (18%)
  local copies, waits for them, and re-layouts  22.8 us (14%)
  starting transfers between devices  18.9 us (12%)
  matrix products  18.1 us (11%)
  other arithmetic  7 us (4%)
    psum x1, blocking collectives, shards(): proj = lax.psum(partial_correlation, ('gz', 'ta'))  63.9 us
    all_to_all x1, waiting for transfers between devices, shards(): lax.all_to_all(outgoing.reshape(device_count, capacity, record_width), ('...  27.9 us
    all_to_all x1, starting transfers between devices, shards(): lax.all_to_all(positions.reshape(device_count, capacity), ('gz', 'ta'), s...  11.1 us
    dot_general x1, matrix products, shards(): jnp.einsum('bkj,bsj->bks', basis, sources, preferred_element_type=jnp.flo...  8.6 us
    dot_general x1, matrix products, shards(): jnp.einsum('bsk,bkj->bsj', combined, basis, preferred_element_type=jnp.fl...  8.59 us
    all_to_all x1, starting transfers between devices, shards(): lax.all_to_all(outgoing.reshape(device_count, capacity, record_width), ('...  7.78 us
    scatter x1, local copies, waits for them, and re-layouts, shards(): coeff_table = jnp.zeros((records, record_width), old_coeffs.dtype).at[arr...  6.73 us
    scatter x1, local copies, waits for them, and re-layouts, shards(): outgoing = jnp.zeros((device_count * capacity, record_width), old_coeffs....  4.86 us
  transfers between devices with their start and end apart: 2, of which 2 were waited for; matrix products, arithmetic and copies ran while one was open for 13% of the time, Pallas kernels for 0%

commit v1 on v0

v1 whole, which is shorter than its diff:
```python
import functools

import jax
import jax.numpy as jnp
from jax import lax
from jax.experimental import pallas as pl
from jax.experimental.pallas import tpu as pltpu
from jax.sharding import PartitionSpec as P

F32 = jnp.float32
BF16 = jnp.bfloat16
MESH = pl.DeviceIdType.MESH

NB = 64
LN = 2 * NB
BV = 3072
S = 12
BLK = 16
MG = 25
MP = 32
GROUPS = 16
RECS = 256
MODES = 400
W = S * LN
PW = W // 3
SAME = 64 * BLK
MIB = 1 << 20


class Place:
    def __init__(self):
        gz = lax.axis_index("gz")
        ta = lax.axis_index("ta")
        self.core = lax.rem(gz, 2)
        self.c = (ta // 4, gz // 2, lax.rem(ta, 4))

    def at(self, axis, d):
        return lax.rem(self.c[axis] + d, 4)

    def device(self, axis, d):
        x, y, z = (self.at(a, d) if a == axis else self.c[a] for a in range(3))
        return (y * 2 + self.core, x * 4 + z)

    def sibling(self):
        x, y, z = self.c
        return (y * 2 + 1 - self.core, x * 4 + z)


def order(p):
    return (p % 3, (p + 1) % 3, (p + 2) % 3)


class Copies:
    def __init__(self, send, recv):
        self.send, self.recv, self.all = send, recv, []

    def start(self, src, dst, device):
        n = len(self.all)
        copy = pltpu.make_async_remote_copy(
            src_ref=src,
            dst_ref=dst,
            send_sem=self.send.at[n],
            recv_sem=self.recv.at[n],
            device_id=device,
            device_id_type=MESH,
        )
        copy.start()
        self.all.append(copy)
        return copy

    def finish(self):
        for copy in self.all:
            copy.wait_send()


def enter(devices):
    barrier = pltpu.get_barrier_semaphore()
    for device in devices:
        pl.semaphore_signal(barrier, inc=1, device_id=device, device_id_type=MESH)
    pl.semaphore_wait(barrier, len(devices))


def partners(place):
    return [place.sibling()] + [place.device(a, d) for a in range(3) for d in (1, 2, 3)]


def low_lanes(shape):
    return lax.broadcasted_iota(jnp.int32, shape, 1) % LN < NB


N_GATHER = 3 * (3 + 4 + 16) + 2 + 3


def gather_kernel(
    basis, sources, keys_col, keys_row, picked, squares, rows_both,
    bbuf, sbuf, prod, stage, table, cols, mine, theirs, got, bsem, ssem, send, recv,
):
    place = Place()
    core = place.core
    for b in range(BLK):
        pltpu.make_async_copy(sources.at[b], sbuf.at[b], ssem.at[b]).start()
        pltpu.make_async_copy(basis.at[b], bbuf.at[b], bsem.at[b]).start()
    enter(partners(place))
    copies = Copies(send, recv)
    cols[0] = keys_col[...]
    rows_both[0] = keys_row[...]
    sib = place.sibling()
    key_copies = [
        copies.start(cols.at[0], cols.at[1], sib),
        copies.start(rows_both.at[0], rows_both.at[1], sib),
    ]

    def block(b, total):
        pltpu.make_async_copy(sources.at[b], sbuf.at[b], ssem.at[b]).wait()
        pltpu.make_async_copy(basis.at[b], bbuf.at[b], bsem.at[b]).wait()
        field = sbuf[b]
        prod[...] = lax.dot_general(
            field, bbuf[b], (((1,), (1,)), ((), ())), preferred_element_type=F32
        )
        a = prod[0:S, :]
        other = pltpu.roll(prod[S : 2 * S, :], NB, 1)
        stage[pl.ds(pl.multiple_of(b * 16, 16), S), :] = other + jnp.where(low_lanes((S, LN)), a, -a)
        wide = field.astype(F32)
        wide = wide * wide
        for t in range(BV // LN):
            total = total + wide[:, t * LN : (t + 1) * LN]
        return total

    squares[...] = lax.fori_loop(0, BLK, block, jnp.zeros((2 * S, LN), F32))

    def row(c3, c2, c1=0):
        return pl.multiple_of(((c3 * 4 + c2) * 4 + c1) * BLK, BLK)

    def rows(p, start, size):
        return table.at[p, pl.ds(start, size), :]

    first = []
    for p in range(3):
        a1, a2, a3 = order(p)
        here = row(place.c[a3], place.c[a2], place.c[a1])
        part = [stage[pl.ds(s, BLK, stride=16), :] for s in range(p * 4, p * 4 + 4)]
        table[p, pl.ds(here, BLK), :] = jnp.concatenate(part, axis=1).astype(BF16)
        first.append(
            [copies.start(rows(p, here, BLK), rows(p, here, BLK), place.device(a1, d)) for d in (1, 3, 2)]
        )

    def both(p, axis, start, size):
        ref = rows(p, start, size)
        return [copies.start(ref, ref, place.device(axis, d)) for d in (1, 3)]

    def forward(p, axis, left, right, size):
        half = size // 2
        a = rows(p, left, half)
        b = rows(p, pl.multiple_of(right + half, BLK), half)
        return [
            copies.start(a, a, place.device(axis, 1)),
            copies.start(b, b, place.device(axis, 3)),
        ]

    def arrived(pair):
        for copy in pair:
            copy.wait_recv()

    line = 4 * BLK
    second, third = [], [[], [], []]
    for p in range(3):
        _, a2, a3 = order(p)
        arrived(first[p])
        start = row(place.c[a3], place.c[a2])
        second.append(both(p, a2, start, line))
        third[p].append(both(p, a3, start, line))
    halves = []
    for p in range(3):
        _, a2, a3 = order(p)
        c3 = place.c[a3]
        arrived(second[p])
        left, right = row(c3, place.at(a2, 3)), row(c3, place.at(a2, 1))
        halves.append(forward(p, a2, left, right, line))
        third[p].append(both(p, a3, left, line))
        third[p].append(both(p, a3, right, line))
    for p in range(3):
        _, a2, a3 = order(p)
        arrived(halves[p])
        third[p].append(both(p, a3, row(place.c[a3], place.at(a2, 2)), line))
    last = [[], [], []]
    for j, d in enumerate((0, 3, 1, 2)):
        for p in range(3):
            _, a2, a3 = order(p)
            c2 = place.at(a2, d)
            arrived(third[p][j])
            last[p].append(
                forward(p, a3, row(place.at(a3, 3), c2), row(place.at(a3, 1), c2), line)
            )
    arrived(key_copies)
    sent = []
    for p in range(3):
        for pair in last[p]:
            arrived(pair)
        lanes = slice(p * PW, (p + 1) * PW)
        ids = lax.broadcasted_iota(jnp.int32, (RECS, SAME), 1) + core * SAME
        for who, out in ((1, theirs), (0, mine)):
            key = cols[who, :, p : p + 1]
            pick = jnp.where(key == ids, 1.0, 0.0).astype(BF16)
            out[p] = jnp.dot(pick, table[p], preferred_element_type=F32).astype(BF16)
            if who == 1:
                sent.append(copies.start(theirs.at[p], got.at[p], sib))
    for p in range(3):
        sent[p].wait_recv()
        picked[:, p * PW : (p + 1) * PW] = mine[p] + got[p]
    copies.finish()


def gather_projections(basis, sources, keys_col, keys_row):
    any_space = pl.BlockSpec(memory_space=pl.ANY)
    vmem = pl.BlockSpec(memory_space=pltpu.VMEM)
    return pl.pallas_call(
        gather_kernel,
        out_shape=(
            jax.ShapeDtypeStruct((RECS, W), BF16),
            jax.ShapeDtypeStruct((2 * S, LN), F32),
            jax.ShapeDtypeStruct((2, 8, RECS), jnp.int32),
        ),
        in_specs=[any_space, any_space, vmem, vmem],
        out_specs=(vmem, vmem, vmem),
        scratch_shapes=[
            pltpu.VMEM((BLK, LN, BV), BF16),
            pltpu.VMEM((BLK, 2 * S, BV), BF16),
            pltpu.VMEM((2 * S, LN), F32),
            pltpu.VMEM((BLK * 16, LN), F32),
            pltpu.VMEM((3, SAME, PW), BF16),
            pltpu.VMEM((2, RECS, LN), jnp.int32),
            pltpu.VMEM((3, RECS, PW), BF16),
            pltpu.VMEM((3, RECS, PW), BF16),
            pltpu.VMEM((3, RECS, PW), BF16),
            pltpu.SemaphoreType.DMA((BLK,)),
            pltpu.SemaphoreType.DMA((BLK,)),
            pltpu.SemaphoreType.DMA((N_GATHER,)),
            pltpu.SemaphoreType.DMA((N_GATHER,)),
        ],
        compiler_params=pltpu.CompilerParams(
            collective_id=1, has_side_effects=True, vmem_limit_bytes=48 * MIB
        ),
    )(basis, sources, keys_col, keys_row)


def spread_records(coeffs, spread):
    for m in range(MG):
        spread[pl.ds(m, RECS, stride=MP), :] = coeffs[:, m * LN : (m + 1) * LN].astype(F32)
    for m in range(MG, MP):
        spread[pl.ds(m, RECS, stride=MP), :] = jnp.zeros((RECS, LN), F32)


def project_kernel(group, coeffs, picked, out, spread, tall, acc):
    spread_records(coeffs, spread)
    for s in range(S):
        tall[pl.ds(s, RECS, stride=16), :] = picked[:, s * LN : (s + 1) * LN].astype(F32)
    for s in range(S, 16):
        tall[pl.ds(s, RECS, stride=16), :] = jnp.zeros((RECS, LN), F32)
    acc[...] = jnp.zeros_like(acc)
    low = low_lanes((16, LN))

    def record(i, carry):
        real = tall[pl.ds(pl.multiple_of(i * 16, 16), 16), :]
        turned = pltpu.roll(real, NB, 1)
        both = jnp.concatenate([real, jnp.where(low, turned, -turned)], axis=0).astype(BF16)
        modes = spread[pl.ds(pl.multiple_of(i * MP, MP), MP), :].astype(BF16)
        term = lax.dot_general(both, modes, (((1,), (1,)), ((), ())), preferred_element_type=F32)
        r = group[i]
        acc[r, :, 0:MP] += term
        return carry

    lax.fori_loop(0, RECS, record, 0, unroll=8)
    for q in range(4):
        total = acc[4 * q]
        for k in range(1, 4):
            total = total + pltpu.roll(acc[4 * q + k], k * MP, 1)
        out[:, q * LN : (q + 1) * LN] = total


def project_records(group, coeffs, picked):
    vmem = pl.BlockSpec(memory_space=pltpu.VMEM)
    return pl.pallas_call(
        project_kernel,
        out_shape=jax.ShapeDtypeStruct((2 * 16, GROUPS * MP), F32),
        in_specs=[pl.BlockSpec(memory_space=pltpu.SMEM), vmem, vmem],
        out_specs=vmem,
        scratch_shapes=[
            pltpu.VMEM((RECS * MP, LN), F32),
            pltpu.VMEM((RECS * 16, LN), F32),
            pltpu.VMEM((GROUPS, 32, LN), F32),
        ],
        compiler_params=pltpu.CompilerParams(vmem_limit_bytes=32 * MIB),
    )(group, coeffs, picked)


def mix_kernel(group, coeffs, weights, out, spread, wt, tall):
    spread_records(coeffs, spread)
    for r in range(GROUPS):
        tile = weights[:, (r // 4) * LN : (r // 4 + 1) * LN]
        wt[r] = tile if r % 4 == 0 else pltpu.roll(tile, LN - (r % 4) * MP, 1)
    low = low_lanes((16, LN))

    def record(i, carry):
        modes = spread[pl.ds(pl.multiple_of(i * MP, MP), MP), :].astype(BF16)
        r = group[i]
        w = wt[r][:, 0:MP].astype(BF16)
        mixed = jnp.dot(w, modes, preferred_element_type=F32)
        turned = pltpu.roll(mixed[16:32, :], NB, 1)
        tall[pl.ds(pl.multiple_of(i * 16, 16), 16), :] = mixed[0:16, :] + jnp.where(low, -turned, turned)
        return carry

    lax.fori_loop(0, RECS, record, 0, unroll=8)
    for s in range(S):
        out[:, s * LN : (s + 1) * LN] = tall[pl.ds(s, RECS, stride=16), :].astype(BF16)


def mix_records(group, coeffs, weights):
    vmem = pl.BlockSpec(memory_space=pltpu.VMEM)
    return pl.pallas_call(
        mix_kernel,
        out_shape=jax.ShapeDtypeStruct((RECS, W), BF16),
        in_specs=[pl.BlockSpec(memory_space=pltpu.SMEM), vmem, vmem],
        out_specs=vmem,
        scratch_shapes=[
            pltpu.VMEM((RECS * MP, LN), F32),
            pltpu.VMEM((GROUPS, 32, LN), F32),
            pltpu.VMEM((RECS * 16, LN), F32),
        ],
        compiler_params=pltpu.CompilerParams(vmem_limit_bytes=32 * MIB),
    )(group, coeffs, weights)


N_SUM = 2 + 27
CUTS = ((0, 8), (8, 16), (24, 8))


def sum_kernel(part, out, half_in, slots, whole, send, recv):
    place = Place()
    sib = place.sibling()
    enter(partners(place))
    copies = Copies(send, recv)
    width = GROUPS * MP // 2
    lanes = pl.ds(pl.multiple_of(place.core * width, width), width)
    other = pl.ds(pl.multiple_of((1 - place.core) * width, width), width)
    copies.start(part.at[:, other], half_in, sib).wait_recv()
    total = part[:, lanes] + half_in[...]
    pieces = [total[a : a + n] for a, n in CUTS]
    for step in range(3):
        waiting = []
        for p, (a, n) in enumerate(CUTS):
            axis = (p + step) % 3
            mine = place.c[axis]
            slots[step, mine, a : a + n, :] = pieces[p]
            ref = slots.at[step, mine, a : a + n, :]
            waiting.append([copies.start(ref, ref, place.device(axis, d)) for d in (1, 3, 2)])
        for p, (a, n) in enumerate(CUTS):
            for copy in waiting[p]:
                copy.wait_recv()
            got = [slots[step, c, a : a + n, :] for c in range(4)]
            pieces[p] = (got[0] + got[1]) + (got[2] + got[3])
    for p, (a, n) in enumerate(CUTS):
        whole[a : a + n, lanes] = pieces[p]
    ref = whole.at[:, lanes]
    copies.start(ref, ref, sib).wait_recv()
    out[...] = whole[...]
    copies.finish()


def sum_everywhere(part):
    vmem = pl.BlockSpec(memory_space=pltpu.VMEM)
    return pl.pallas_call(
        sum_kernel,
        out_shape=jax.ShapeDtypeStruct(part.shape, F32),
        in_specs=[vmem],
        out_specs=vmem,
        scratch_shapes=[
            pltpu.VMEM((32, GROUPS * MP // 2), F32),
            pltpu.VMEM((3, 4, 32, GROUPS * MP // 2), F32),
            pltpu.VMEM((32, GROUPS * MP), F32),
            pltpu.SemaphoreType.DMA((N_SUM,)),
            pltpu.SemaphoreType.DMA((N_SUM,)),
        ],
        compiler_params=pltpu.CompilerParams(collective_id=2, has_side_effects=True),
    )(part)


N_REDUCE = 1 + 3 * (4 + 4 + 3)


def reduce_kernel(
    mixed, keys, out, both, x, far_out, far_in, near_out, near_in,
    far2_out, far2_in, near2_out, near2_in, own_out, own_in, send, recv,
):
    place = Place()
    core = place.core
    sib = place.sibling()
    enter(partners(place))
    copies = Copies(send, recv)
    both[0] = mixed[...]
    exchange = copies.start(both.at[0], both.at[1], sib)
    exchange.wait_recv()
    plane, line = 16 * BLK, 4 * BLK

    def partial(p, c3):
        base = core * SAME + c3 * plane
        ids = lax.broadcasted_iota(jnp.int32, (plane, RECS), 0) + base
        total = None
        for who in range(2):
            pick = jnp.where(keys[who, p : p + 1, :] == ids, 1.0, 0.0).astype(BF16)
            term = jnp.dot(pick, both[who, :, p * PW : (p + 1) * PW], preferred_element_type=F32)
            total = term if total is None else total + term
        return total

    far = []
    for p in range(3):
        a3 = order(p)[2]
        far_out[p] = partial(p, place.at(a3, 2)).astype(BF16)
        half = plane // 2
        far.append([
            copies.start(far_out.at[p, 0:half, :], far_in.at[p, 0], place.device(a3, 1)),
            copies.start(far_out.at[p, half:plane, :], far_in.at[p, 1], place.device(a3, 3)),
        ])
    near = []
    for p in range(3):
        a3 = order(p)[2]
        half = plane // 2
        pair = []
        for k, d in enumerate((1, 3)):
            total = partial(p, place.at(a3, d))
            far[p][k].wait_recv()
            more = far_in[p, k].astype(F32)
            if k == 0:
                near_out[p, k, 0:half, :] = (total[0:half] + more).astype(BF16)
                near_out[p, k, half:plane, :] = total[half:plane].astype(BF16)
            else:
                near_out[p, k, 0:half, :] = total[0:half].astype(BF16)
                near_out[p, k, half:plane, :] = (total[half:plane] + more).astype(BF16)
            pair.append(copies.start(near_out.at[p, k], near_in.at[p, k], place.device(a3, d)))
        near.append(pair)
    for p in range(3):
        x[p] = partial(p, place.c[order(p)[2]])
    far2 = []
    for p in range(3):
        a2 = order(p)[1]
        near[p][0].wait_recv()
        near[p][1].wait_recv()
        x[p] = x[p] + near_in[p, 0].astype(F32) + near_in[p, 1].astype(F32)
        c = pl.multiple_of(place.at(a2, 2) * line, line)
        half = line // 2
        far2_out[p] = x[p, pl.ds(c, line), :].astype(BF16)
        far2.append([
            copies.start(far2_out.at[p, 0:half, :], far2_in.at[p, 0], place.device(a2, 1)),
            copies.start(far2_out.at[p, half:line, :], far2_in.at[p, 1], place.device(a2, 3)),
        ])
    near2 = []
    for p in range(3):
        a2 = order(p)[1]
        half = line // 2
        pair = []
        for k, d in enumerate((1, 3)):
            far2[p][k].wait_recv()
            total = x[p, pl.ds(pl.multiple_of(place.at(a2, d) * line, line), line), :]
            more = far2_in[p, k].astype(F32)
            if k == 0:
                near2_out[p, k, 0:half, :] = (total[0:half] + more).astype(BF16)
                near2_out[p, k, half:line, :] = total[half:line].astype(BF16)
            else:
                near2_out[p, k, 0:half, :] = total[0:half].astype(BF16)
                near2_out[p, k, half:line, :] = (total[half:line] + more).astype(BF16)
            pair.append(copies.start(near2_out.at[p, k], near2_in.at[p, k], place.device(a2, d)))
        near2.append(pair)
    last = []
    for p in range(3):
        a1, a2, _ = order(p)
        near2[p][0].wait_recv()
        near2[p][1].wait_recv()
        total = x[p, pl.ds(pl.multiple_of(place.c[a2] * line, line), line), :]
        total = total + near2_in[p, 0].astype(F32) + near2_in[p, 1].astype(F32)
        x[p, 0:line, :] = total
        trio = []
        for k, d in enumerate((1, 3, 2)):
            c = pl.multiple_of(place.at(a1, d) * BLK, BLK)
            own_out[p, k] = x[p, pl.ds(c, BLK), :].astype(BF16)
            trio.append(copies.start(own_out.at[p, k], own_in.at[p, k], place.device(a1, d)))
        last.append(trio)
    for p in range(3):
        a1 = order(p)[0]
        total = x[p, pl.ds(pl.multiple_of(place.c[a1] * BLK, BLK), BLK), :]
        for k in range(3):
            last[p][k].wait_recv()
            total = total + own_in[p, k].astype(F32)
        out[:, p * PW : (p + 1) * PW] = total
    copies.finish()


def reduce_to_owners(mixed, keys):
    vmem = pl.BlockSpec(memory_space=pltpu.VMEM)
    plane, line = 16 * BLK, 4 * BLK
    return pl.pallas_call(
        reduce_kernel,
        out_shape=jax.ShapeDtypeStruct((BLK, W), F32),
        in_specs=[vmem, vmem],
        out_specs=vmem,
        scratch_shapes=[
            pltpu.VMEM((2, RECS, W), BF16),
            pltpu.VMEM((3, plane, PW), F32),
            pltpu.VMEM((3, plane, PW), BF16),
            pltpu.VMEM((3, 2, plane // 2, PW), BF16),
            pltpu.VMEM((3, 2, plane, PW), BF16),
            pltpu.VMEM((3, 2, plane, PW), BF16),
            pltpu.VMEM((3, line, PW), BF16),
            pltpu.VMEM((3, 2, line // 2, PW), BF16),
            pltpu.VMEM((3, 2, line, PW), BF16),
            pltpu.VMEM((3, 2, line, PW), BF16),
            pltpu.VMEM((3, 3, BLK, PW), BF16),
            pltpu.VMEM((3, 3, BLK, PW), BF16),
            pltpu.SemaphoreType.DMA((N_REDUCE,)),
            pltpu.SemaphoreType.DMA((N_REDUCE,)),
        ],
        compiler_params=pltpu.CompilerParams(
            collective_id=3, has_side_effects=True, vmem_limit_bytes=32 * MIB
        ),
    )(mixed, keys)


def guess_kernel(g, basis, out, tall, comb):
    b = pl.program_id(0)

    @pl.when(b == 0)
    def _():
        for s in range(S):
            tall[pl.ds(s, BLK, stride=16), :] = g[:, s * LN : (s + 1) * LN]

    mine = tall[pl.ds(pl.multiple_of(b * 16, 16), S), :]
    comb[0:S, :] = jnp.where(low_lanes((S, LN)), mine, -mine)
    comb[S : 2 * S, :] = pltpu.roll(mine, NB, 1)
    out[...] = jnp.dot(comb[...].astype(BF16), basis[0], preferred_element_type=F32)[None]


def make_guesses(g, basis):
    return pl.pallas_call(
        guess_kernel,
        out_shape=jax.ShapeDtypeStruct((BLK, 2 * S, BV), F32),
        grid=(BLK,),
        in_specs=[
            pl.BlockSpec((BLK, W), lambda b: (0, 0)),
            pl.BlockSpec((1, LN, BV), lambda b: (b, 0, 0)),
        ],
        out_specs=pl.BlockSpec((1, 2 * S, BV), lambda b: (b, 0, 0)),
        scratch_shapes=[
            pltpu.VMEM((BLK * 16, LN), F32),
            pltpu.VMEM((2 * S, LN), F32),
        ],
        compiler_params=pltpu.CompilerParams(vmem_limit_bytes=32 * MIB),
    )(g, basis)


def keys_of(dest_owner, new_pos):
    core = (dest_owner // 16) % 2
    c = ((dest_owner // 4) % 4, dest_owner // 32, dest_owner % 4)
    found = []
    for p in range(3):
        a1, a2, a3 = order(p)
        slot = ((core * 4 + c[a3]) * 4 + c[a2]) * 4 + c[a1]
        found.append(slot * BLK + new_pos // GROUPS)
    return jnp.stack(found)


def shards(basis, sources, old_coeffs, eigenvalues, dest_owner, new_pos):
    keys = keys_of(dest_owner, new_pos)
    group = new_pos % GROUPS
    keys_row = jnp.pad(keys, ((0, 5), (0, 0)))
    keys_col = jnp.pad(keys.T, ((0, 0), (0, LN - 3)))
    picked, squares, rows_both = gather_projections(basis, sources, keys_col, keys_row)
    part = project_records(group, old_coeffs, picked)
    local = jnp.sum(squares, axis=1)
    local = jnp.pad(local[:S] + local[S:], (0, 4))
    part = part.at[:, MG].set(jnp.concatenate([local, local]))
    total = sum_everywhere(part)
    norm_sq = total[:, MG]
    scale = jnp.sqrt(jnp.float32(2 * 128 * BLK * BV)) * lax.rsqrt(norm_sq + 1e-06)
    scaled = (total * scale[:, None]).reshape(32, GROUPS, MP)[:, :, :MG]
    correlations = jnp.concatenate([scaled[0:S], scaled[16 : 16 + S]]).reshape(2 * S, MODES).T
    weights = (scaled / eigenvalues.reshape(1, GROUPS, MG)).astype(BF16).astype(F32)
    weights = jnp.pad(weights, ((0, 0), (0, 0), (0, MP - MG))).reshape(32, GROUPS * MP)
    mixed = mix_records(group, old_coeffs, weights)
    g = reduce_to_owners(mixed, rows_both)
    return make_guesses(g, basis), correlations


def solution(mesh):
    in_specs = (
        P(("gz", "ta"), None, None),
        P(("gz", "ta"), None, None),
        P(("gz", "ta"), None),
        P(),
        P(("gz", "ta")),
        P(("gz", "ta")),
    )
    out_specs = (P(("gz", "ta"), None, None), P())
    return jax.shard_map(shards, mesh=mesh, in_specs=in_specs, out_specs=out_specs, check_vma=False)
```

time: 163 us -> 140 us (0.86)
  Pallas kernels: 0 us -> 125 us
  blocking collectives: 63.9 us -> 0 us
  waiting for transfers between devices: 30.1 us -> 0 us
  starting transfers between devices: 18.9 us -> 0 us
  matrix products: 18.1 us -> 0 us
  local copies, waits for them, and re-layouts: 22.8 us -> 9.2 us
  other arithmetic: 7 us -> 4.95 us
    pallas_call x0 -> x6, Pallas kernels: none -> 125 us  [the longest x1 42.4 us: gather_projections(): pl.pallas_call(gather_kernel, out_shape=(jax.ShapeDtypeStruct((RECS, W),...]
    psum x1 -> x0, blocking collectives: 63.9 us -> none  [shards(): proj = lax.psum(partial_correlation, ('gz', 'ta'))]
    all_to_all x2 -> x0, waiting for transfers between devices: 30.1 us -> none  [the longest x1 27.9 us: shards(): lax.all_to_all(outgoing.reshape(device_count, capacity, record_width), ('...]
    all_to_all x2 -> x0, starting transfers between devices: 18.9 us -> none  [the longest x1 11.1 us: shards(): lax.all_to_all(positions.reshape(device_count, capacity), ('gz', 'ta'), s...]
    dot_general x4 -> x0, matrix products: 18.1 us -> none  [the longest x1 8.6 us: shards(): jnp.einsum('bkj,bsj->bks', basis, sources, preferred_element_type=jnp.flo...]
    scatter x3 -> x1, local copies, waits for them, and re-layouts: 13.1 us -> 0.31 us  [shards(): part = part.at[:, MG].set(jnp.concatenate([local, local]))]
    unnamed x11 -> x9, local copies, waits for them, and re-layouts: 0.64 us -> 6.99 us
    reshape x4 -> x3, local copies, waits for them, and re-layouts: 6.96 us -> 1 us  [the longest x1 0.75 us: shards(): jnp.concatenate([scaled[0:S], scaled[16:16 + S]]).reshape(2 * S, MODES)]
  transfers between devices with their start and end apart: 2 -> 0, of which waited for: 2 -> 0; matrix products, arithmetic and copies ran while one was open for 13% -> 0% of each run, Pallas kernels for 0% -> 0%
where the time goes in v1:
time: 140 us
  Pallas kernels  125 us (89%)
  local copies, waits for them, and re-layouts  9.2 us (7%)
  other arithmetic  4.95 us (4%)
    pallas_call x1, Pallas kernels, gather_projections(): pl.pallas_call(gather_kernel, out_shape=(jax.ShapeDtypeStruct((RECS, W),...  42.4 us
    pallas_call x1, Pallas kernels, reduce_to_owners(): pl.pallas_call(reduce_kernel, out_shape=jax.ShapeDtypeStruct((BLK, W), F3...  30.4 us
    pallas_call x1, Pallas kernels, sum_everywhere(): pl.pallas_call(sum_kernel, out_shape=jax.ShapeDtypeStruct(part.shape, F32...  17.5 us
    pallas_call x1, Pallas kernels, project_records(): pl.pallas_call(project_kernel, out_shape=jax.ShapeDtypeStruct((2 * 16, GR...  13.5 us
    pallas_call x1, Pallas kernels, mix_records(): pl.pallas_call(mix_kernel, out_shape=jax.ShapeDtypeStruct((RECS, W), BF16...  12.5 us
    pallas_call x1, Pallas kernels, make_guesses(): pl.pallas_call(guess_kernel, out_shape=jax.ShapeDtypeStruct((BLK, 2 * S,...  8.42 us
    unnamed x9, local copies, waits for them, and re-layouts  6.99 us

profile of v1, /device:TPU:0, one launch (start us, length us, event | category | flops | bytes accessed | tf_op | source)
XLA Modules:
  0.0 139.7 jit_solution(9616511785001036608)
XLA Ops:
  0.6 0.6 compare_reduce_fusion
  1.3 0.7 multiply_add_fusion.2
  2.0 0.7 multiply_add_fusion.1
  2.7 0.8 div.66
  3.5 0.1 copy.12
  3.7 0.0 copy-start.2
  3.7 1.7 %copy-done.2 = bf16[16,24,3072]{2,1,0:T(8,128)(2,1)S(1)} copy-done((bf16[16,24,3072]{2,1,0:T(8,128)(2,1)S(1)}, bf16[16,24,3072]{2,1,0:T(8,128)(2,1)}, u32[]{:S(2)}) %copy-start.2) | copy-done | bytes 2359320
  5.3 0.0 copy-start.1
  5.3 42.4 %shard_map.77 = (bf16[256,1536]{1,0:T(8,128)(2,1)S(1)}, f32[24,128]{1,0:T(8,128)S(1)}, s32[2,8,256]{2,1,0:T(8,128)S(1)}) custom-call(bf16[16,128,3072]{2,1,0:T(8,128)(2,1)} %basis.3, bf16[16,24,3072]{2,1,0:T(8,128)(2,1)S(1)} %copy-done.2, s32[256,128]{1,0:T(8,128)S(1)} %pad.19.clone.keys_col, s32[8,256]{1,0:T(8,128)S(1)} %pad.20.keys_row), custom_call_target="tpu_custom_call" | custom-call | tf_op jit(solution)/shard_map/pallas_call | solution.py:216
  47.8 0.0 copy-done.1
  47.8 13.5 %shard_map.78 = f32[32,512]{1,0:T(8,128)S(1)} custom-call(s32[256]{0:T(256)S(1)} %get-tuple-element.30.group, bf16[256,3200]{1,0:T(8,128)(2,1)S(1)} %copy-done.1, bf16[256,1536]{1,0:T(8,128)(2,1)S(1)} %get-tuple-element.17.picked), custom_call_target="tpu_custom_call" | custom-call | tf_op jit(solution)/shard_map/pallas_call | solution.py:282
  61.3 0.1 reduce_sum.9
  61.4 0.1 slice_add_fusion
  61.4 0.1 maximum_bitcast_fusion
  61.5 0.1 copy.11
  61.6 0.7 slice_select_fusion
  62.3 0.3 scatter.4.part
  62.7 0.0 copy-start.3
  62.7 0.6 copy-done.3
  63.3 17.5 %shard_map.79 = f32[32,512]{1,0:T(8,128)} custom-call(f32[32,512]{1,0:T(8,128)} %copy-done.3), custom_call_target="tpu_custom_call" | custom-call | tf_op jit(solution)/shard_map/pallas_call | solution.py:371
  80.8 0.9 multiply_reduce_fusion
  81.7 0.9 broadcast_multiply_fusion
  82.6 0.1 reshape.45
  82.8 0.8 reshape.48
  83.6 0.1 reshape.50.weights
  83.7 12.5 %shard_map.80.mixed = bf16[256,1536]{1,0:T(8,128)(2,1)S(1)} custom-call(s32[256]{0:T(256)S(1)} %get-tuple-element.30.group, bf16[256,3200]{1,0:T(8,128)(2,1)S(1)} %copy-done.1, f32[32,512]{1,0:T(8,128)S(1)} %reshape.50.weights), custom_call_target="tpu_custom_call" | custom-call | tf_op jit(solution)/shard_map/pallas_call | solution.py:319
  96.3 30.4 %shard_map.81.g = f32[16,1536]{1,0:T(8,128)S(1)} custom-call(bf16[256,1536]{1,0:T(8,128)(2,1)S(1)} %shard_map.80.mixed, s32[2,8,256]{2,1,0:T(8,128)S(1)} %get-tuple-element.19.keys), custom_call_target="tpu_custom_call" | custom-call | tf_op jit(solution)/shard_map/pallas_call | solution.py:499
  126.7 0.0 copy-start
  126.7 4.6 %copy-done = bf16[16,128,3072]{2,1,0:T(8,128)(2,1)S(1)} copy-done((bf16[16,128,3072]{2,1,0:T(8,128)(2,1)S(1)}, bf16[16,128,3072]{2,1,0:T(8,128)(2,1)}, u32[]{:S(2)}) %copy-start) | copy-done | bytes 12582936
  131.3 8.4 %shard_map.82 = f32[16,24,3072]{2,1,0:T(8,128)} custom-call(f32[16,1536]{1,0:T(8,128)S(1)} %shard_map.81.g, bf16[16,128,3072]{2,1,0:T(8,128)(2,1)S(1)} %copy-done), custom_call_target="tpu_custom_call" | custom-call | tf_op jit(solution)/shard_map/pallas_call | solution.py:541
  (8 shorter events, 0.1 us)
Async XLA Ops:
  3.7 1.7 %copy-start.2 = (bf16[16,24,3072]{2,1,0:T(8,128)(2,1)S(1)}, bf16[16,24,3072]{2,1,0:T(8,128)(2,1)}, u32[]{:S(2)}) copy-start(bf16[16,24,3072]{2,1,0:T(8,128)(2,1)} %sources.1) | copy-start | bytes 7077892
  5.3 42.4 %copy-start.1 = (bf16[256,3200]{1,0:T(8,128)(2,1)S(1)}, bf16[256,3200]{1,0:T(8,128)(2,1)}, u32[]{:S(2)}) copy-start(bf16[256,3200]{1,0:T(8,128)(2,1)} %coeffs.3) | copy-start | bytes 4915204
  62.7 0.6 copy-start.3
  126.7 4.6 %copy-start = (bf16[16,128,3072]{2,1,0:T(8,128)(2,1)S(1)}, bf16[16,128,3072]{2,1,0:T(8,128)(2,1)}, u32[]{:S(2)}) copy-start(bf16[16,128,3072]{2,1,0:T(8,128)(2,1)} %basis.3) | copy-start | bytes 37748740

commit v2 on v0

v2 whole, which is shorter than its diff:
```python
import jax
import jax.numpy as jnp
from jax import lax
from jax.experimental import pallas as pl
from jax.experimental.pallas import tpu as pltpu
from jax.sharding import PartitionSpec as P

F32 = jnp.float32
BF16 = jnp.bfloat16
I32 = jnp.int32
MESH = pl.DeviceIdType.MESH

NB = 64
LN = 2 * NB
BV = 3072
S = 12
BLK = 16
MG = 25
MP = 32
GROUPS = 16
RECS = 256
MODES = 400
H = 2
SH = S // H
PARTS = 3 * H
PW = 2 * LN
HW = SH * LN
RR = 16
SAME = 64 * BLK
PLANE, LINE = 16 * BLK, 4 * BLK
MIB = 1 << 20
N_COPIES = 1 + PARTS * 22 + PARTS + H * (14 + 6 + 14) + H + PARTS * 10


class Place:
    def __init__(self):
        gz = lax.axis_index("gz")
        ta = lax.axis_index("ta")
        self.core = lax.rem(gz, 2)
        self.c = (ta // 4, gz // 2, lax.rem(ta, 4))

    def at(self, axis, d):
        return lax.rem(self.c[axis] + d, 4)

    def device(self, axis, d, flip=False):
        x, y, z = (self.at(a, d) if a == axis else self.c[a] for a in range(3))
        return (y * 2 + (1 - self.core if flip else self.core), x * 4 + z)


def order(q):
    return (q % 3, (q + 1) % 3, (q + 2) % 3)


class Copies:
    def __init__(self, send, recv):
        self.send, self.recv, self.all = send, recv, []

    def start(self, src, dst, device):
        n = len(self.all)
        copy = pltpu.make_async_remote_copy(
            src_ref=src,
            dst_ref=dst,
            send_sem=self.send.at[n],
            recv_sem=self.recv.at[n],
            device_id=device,
            device_id_type=MESH,
        )
        copy.start()
        self.all.append(copy)
        return copy

    def finish(self):
        for copy in self.all:
            copy.wait_send()


def arrived(copies):
    for copy in copies:
        copy.wait_recv()


def iota(shape, axis):
    return lax.broadcasted_iota(I32, shape, axis)


def low_lanes(shape):
    return iota(shape, 1) % LN < NB


def spread_lanes(x):
    x = x + pltpu.roll(x, 2 * MP, 1)
    return x + pltpu.roll(x, MP, 1)


def kernel(
    basis, sources, coeffs_in, owner_in, pos_in, pos, eig_in,
    guesses, corr_out,
    bbuf, sbuf, prod, stage, sq, table, idsb, lane_group, eig, terms, coeffs, kbig, kcol, pick, pick_t, wide, modes,
    mine, theirs, got, xs, pay, ar1, ar2, ar3, corr, wt, tall, both,
    far_out, far_in, near_out, near_in, x, line_out, line_in, own_out, own_in, gs, comb, gout,
    bsem, ssem, osem, csem, send, recv,
):
    place = Place()
    core = place.core
    sib = place.device(0, 0, True)
    copies = Copies(send, recv)

    def pair_load(j):
        at = pl.ds(j * 2, 2)
        return (
            pltpu.make_async_copy(sources.at[at], sbuf.at[at], ssem.at[j]),
            pltpu.make_async_copy(basis.at[at], bbuf.at[at], bsem.at[j]),
        )

    for j in range(3):
        for copy in pair_load(j):
            copy.start()
    load_coeffs = pltpu.make_async_copy(coeffs_in, coeffs, csem)
    load_coeffs.start()
    barrier = pltpu.get_barrier_semaphore()
    friends = [sib] + [place.device(a, d, f) for a in range(3) for d in (1, 2, 3) for f in (False, True)]
    for friend in friends:
        pl.semaphore_signal(barrier, inc=1, device_id=friend, device_id_type=MESH)

    low12 = low_lanes((S, LN))

    def block_pair(j, total):
        for copy in pair_load(j):
            copy.wait()

        @pl.when(j + 3 < BLK // 2)
        def _():
            for copy in pair_load(j + 3):
                copy.start()

        at = pl.ds(j * 2, 2)
        field = sbuf[at].reshape(4 * S, BV)
        vectors = bbuf[at].reshape(2 * LN, BV)
        prod[...] = lax.dot_general(
            field, vectors, (((1,), (1,)), ((), ())), preferred_element_type=F32
        )
        for k in range(2):
            lanes = slice(k * LN, (k + 1) * LN)
            a = prod[2 * S * k : 2 * S * k + S, lanes]
            b = pltpu.roll(prod[2 * S * k + S : 2 * S * k + 2 * S, lanes], NB, 1)
            stage[pl.ds(pl.multiple_of((j * 2 + k) * 16, 16), S), :] = b + jnp.where(low12, a, -a)
        wide_field = field.astype(F32)
        wide_field = wide_field * wide_field
        for t in range(BV // LN):
            total = total + wide_field[:, t * LN : (t + 1) * LN]
        return total

    total = lax.fori_loop(0, BLK // 2, block_pair, jnp.zeros((4 * S, LN), F32))
    sq[...] = jnp.broadcast_to(
        jnp.sum(total[0 : 2 * S] + total[2 * S : 4 * S], axis=1, keepdims=True), (2 * S, LN)
    )
    pl.semaphore_wait(barrier, len(friends))

    def row(c3, c2, c1=0):
        return pl.multiple_of(((c3 * 4 + c2) * 4 + c1) * BLK, BLK)

    def rows(q, start, size):
        return table.at[q, pl.ds(start, size), :]

    first, second, third, last = {}, {}, {}, {}

    def to_axis(q, axis, start, size, ds):
        ref = rows(q, start, size)
        return [copies.start(ref, ref, place.device(axis, d)) for d in ds]

    def ag1(q):
        a1, a2, a3 = order(q)
        here = row(place.c[a3], place.c[a2], place.c[a1])
        s = q * 2
        own = [stage[pl.ds(s + k, BLK, stride=16), :] for k in range(2)]
        table[q, pl.ds(here, BLK), :] = jnp.concatenate(own, axis=1).astype(BF16)
        first[q] = to_axis(q, a1, here, BLK, (1, 3, 2))

    def ag2(q):
        _, a2, a3 = order(q)
        arrived(first[q])
        second[q] = to_axis(q, a2, row(place.c[a3], place.c[a2]), LINE, (1, 3, 2))

    def ag3(q, d):
        _, a2, a3 = order(q)
        if d:
            second[q][{3: 0, 1: 1, 2: 2}[d]].wait_recv()
        third[q, d] = to_axis(q, a3, row(place.c[a3], place.at(a2, d)), LINE, (1, 3))

    def ag_forward(q, d):
        _, a2, a3 = order(q)
        arrived(third[q, d])
        c2 = place.at(a2, d)
        half = LINE // 2
        a = rows(q, row(place.at(a3, 3), c2), half)
        b = rows(q, pl.multiple_of(row(place.at(a3, 1), c2) + half, BLK), half)
        last[q, d] = [
            copies.start(a, a, place.device(a3, 1)),
            copies.start(b, b, place.device(a3, 3)),
        ]

    def make_keys():
        kbig[...] = jnp.zeros_like(kbig)
        for who in range(2):
            owner, at = idsb[who, 0:1, :], idsb[who, 1:2, :]
            c = ((owner >> 2) & 3, owner >> 5, owner & 3)
            same = ((owner >> 4) & 1) == core
            for p in range(3):
                a1, a2, a3 = order(p)
                key = ((c[a3] * 4 + c[a2]) * 4 + c[a1]) * BLK + (at >> 4)
                key = jnp.where(same, key, -1)
                kbig[who * 3 + p : who * 3 + p + 1, :] = key.astype(F32)
        kcol[...] = kbig[...].T

    def make_picks():
        wide_ids = iota((RECS, SAME), 1).astype(F32)
        for who in range(2):
            for p in range(3):
                k = who * 3 + p
                pick[p, who] = jnp.where(kcol[:, k : k + 1] == wide_ids, 1.0, 0.0).astype(BF16)

    def make_picks_t():
        tall_ids = iota((SAME, RECS), 0).astype(F32)
        for who in range(2):
            for p in range(3):
                k = who * 3 + p
                pick_t[p, :, who * RECS : (who + 1) * RECS] = jnp.where(
                    kbig[k : k + 1, :] == tall_ids, 1.0, 0.0
                ).astype(BF16)

    def make_modes():
        for m in range(MG):
            wide[pl.ds(m, RECS, stride=MP), :] = coeffs[:, m * LN : (m + 1) * LN].astype(F32)
        for m in range(MG, MP):
            wide[pl.ds(m, RECS, stride=MP), :] = jnp.zeros((RECS, LN), F32)
        modes[...] = wide[...].astype(BF16)

    def make_tables():
        i = iota((RECS // 4, RECS), 1)
        group = jnp.where(i // 4 == iota((RECS // 4, RECS), 0), pos_in[...] & (GROUPS - 1), 0)
        lanes = iota((RECS, LN), 0) % 4 == iota((RECS, LN), 1) // MP
        lane_group[...] = jnp.dot(
            group.astype(F32).astype(BF16),
            jnp.where(lanes, 1.0, 0.0).astype(BF16),
            preferred_element_type=F32,
        )
        wide_eig = jnp.concatenate([eig_in[...], jnp.ones((1, GROUPS * MP - MODES), F32)], axis=1)
        lane = iota((1, GROUPS * MP), 1)
        padded = jnp.full((1, GROUPS * MP), jnp.inf, F32)
        for r in range(GROUPS):
            moved = pltpu.roll(wide_eig, r * (MP - MG), 1) if r else wide_eig
            padded = jnp.where((lane // MP == r) & (lane % MP < MG), moved, padded)
        eig[...] = jnp.broadcast_to(padded, eig.shape)

    exchange = {}

    def gather(h):
        for p in range(3):
            q = h * 3 + p
            for d in range(4):
                arrived(last[q, d])
            theirs[q] = jnp.dot(pick[p, 1], table[q], preferred_element_type=F32).astype(BF16)
            exchange[q] = copies.start(theirs.at[q], got.at[q], sib)
        for p in range(3):
            q = h * 3 + p
            mine[q] = jnp.dot(pick[p, 0], table[q], preferred_element_type=F32).astype(BF16)

    low_rec = low_lanes((RECS, LN))
    group32 = iota((RR, LN), 1) // MP

    def project(h):
        for s in (6, 7, 14, 15):
            xs[pl.ds(s, RECS, stride=RR), :] = jnp.zeros((RECS, LN), F32)
        for p in range(3):
            q = h * 3 + p
            exchange[q].wait_recv()
            both_cores = mine[q].astype(F32) + got[q].astype(F32)
            for k in range(2):
                real = both_cores[:, k * LN : (k + 1) * LN]
                turned = pltpu.roll(real, NB, 1)
                xs[pl.ds(2 * p + k, RECS, stride=RR), :] = real
                xs[pl.ds(8 + 2 * p + k, RECS, stride=RR), :] = jnp.where(low_rec, turned, -turned)

        def eight(g, carry):
            left = xs[pl.ds(pl.multiple_of(g * 8 * RR, 8 * RR), 8 * RR), :].astype(BF16)
            right = modes[pl.ds(pl.multiple_of(g * 8 * MP, 8 * MP), 8 * MP), :]
            out = lax.dot_general(left, right, (((1,), (1,)), ((), ())), preferred_element_type=F32)
            for t in range(2):
                lanes = slice(t * LN, (t + 1) * LN)
                term = out[4 * t * RR : (4 * t + 1) * RR, lanes]
                for k in range(1, 4):
                    a = 4 * t + k
                    term = jnp.where(group32 == k, out[a * RR : (a + 1) * RR, lanes], term)
                terms[pl.ds(pl.multiple_of((g * 2 + t) * RR, RR), RR), :] = term
            return carry

        lax.fori_loop(0, RECS // 8, eight, 0, unroll=4)

        def four(g, acc):
            term = terms[pl.ds(pl.multiple_of(g * RR, RR), RR), :]
            whose = lane_group[pl.ds(g, 1), :]
            return tuple(acc[r] + jnp.where(whose == float(r), term, 0.0) for r in range(GROUPS))

        acc = lax.fori_loop(0, RECS // 4, four, (jnp.zeros((RR, LN), F32),) * GROUPS, unroll=4)
        for t in range(4):
            tile = spread_lanes(acc[4 * t])
            for k in range(1, 4):
                tile = jnp.where(group32 == k, spread_lanes(acc[4 * t + k]), tile)
            pay[h, :, t * LN : (t + 1) * LN] = tile
        norm = sq[h * SH : (h + 1) * SH, :] + sq[S + h * SH : S + (h + 1) * SH, :]
        lane = iota((SH, LN), 1)
        for base in (0, 8):
            old = pay[h, base : base + SH, 0:LN]
            pay[h, base : base + SH, 0:LN] = jnp.where(lane == MG, norm, old)

    steps = {}
    half_lanes = GROUPS * MP // 2

    def axis_of(h, v, step):
        return (v + h + step) % 3

    def sum1(h):
        for v in range(2):
            axis = axis_of(h, v, 0)
            slot = place.c[axis] * 2 + core
            piece = slice(8 * v, 8 * v + 8)
            ours = pl.ds(pl.multiple_of(core * half_lanes, half_lanes), half_lanes)
            other = pl.ds(pl.multiple_of((1 - core) * half_lanes, half_lanes), half_lanes)
            ar1[h, v, slot] = pay[h, piece, ours]
            dst = ar1.at[h, v, slot]
            steps[1, h, v] = [
                copies.start(pay.at[h, piece, other if f else ours], dst, place.device(axis, d, f))
                for d in (0, 1, 3, 2) for f in (False, True) if d or f
            ]

    def sum2(h):
        for v in range(2):
            arrived(steps[1, h, v])
            total = ar1[h, v, 0]
            for k in range(1, 8):
                total = total + ar1[h, v, k]
            axis = axis_of(h, v, 1)
            slot = place.c[axis]
            ar2[h, v, slot] = total
            ref = ar2.at[h, v, slot]
            steps[2, h, v] = [copies.start(ref, ref, place.device(axis, d)) for d in (1, 3, 2)]

    def sum3(h):
        for v in range(2):
            arrived(steps[2, h, v])
            total = (ar2[h, v, 0] + ar2[h, v, 1]) + (ar2[h, v, 2] + ar2[h, v, 3])
            axis = axis_of(h, v, 2)
            slot = place.c[axis]
            ar3[h, v, core, slot] = total
            ref = ar3.at[h, v, core, slot]
            steps[3, h, v] = [
                copies.start(ref, ref, place.device(axis, d, f))
                for d in (0, 1, 3, 2) for f in (False, True) if d or f
            ]

    def weigh(h):
        for v in range(2):
            arrived(steps[3, h, v])
        scale = None
        for t in range(4):
            k, lanes = t // 2, slice((t % 2) * LN, (t % 2 + 1) * LN)
            tile = jnp.concatenate(
                [
                    (ar3[h, v, k, 0, :, lanes] + ar3[h, v, k, 1, :, lanes])
                    + (ar3[h, v, k, 2, :, lanes] + ar3[h, v, k, 3, :, lanes])
                    for v in range(2)
                ],
                axis=0,
            )
            if scale is None:
                norm_sq = tile[:, MG : MG + 1]
                cells = jnp.float32(2 * 128 * BLK * BV)
                scale = jnp.sqrt(cells) * lax.rsqrt(norm_sq + 1e-06)
            tile = tile * scale
            corr[h * SH : (h + 1) * SH, t * LN : (t + 1) * LN] = tile[0:SH]
            corr[S + h * SH : S + (h + 1) * SH, t * LN : (t + 1) * LN] = tile[8 : 8 + SH]
            weights = tile / eig[0:1, t * LN : (t + 1) * LN]
            for k in range(4):
                wt[h, 4 * t + k] = spread_lanes(jnp.where(group32 == k, weights, 0.0)).astype(BF16)

    def mix(h):
        low8 = low_lanes((8, LN))
        zero = jnp.zeros((RR, LN), BF16)

        def eight(g, carry):
            strips = []
            for a in range(8):
                group = pos[g * 8 + a] & (GROUPS - 1)
                strip = jnp.where(group32 == a % 4, wt[h, group], zero)
                pair = [strip, zero] if a < 4 else [zero, strip]
                strips.append(jnp.concatenate(pair, axis=1))
            left = jnp.concatenate(strips, axis=0)
            right = modes[pl.ds(pl.multiple_of(g * 8 * MP, 8 * MP), 8 * MP), :]
            out = jnp.dot(left, right, preferred_element_type=F32)
            for a in range(8):
                real, imag = out[a * RR : a * RR + 8], out[a * RR + 8 : a * RR + 16]
                turned = pltpu.roll(imag, NB, 1)
                at = pl.ds(pl.multiple_of((g * 8 + a) * 8, 8), 8)
                tall[at, :] = real + jnp.where(low8, -turned, turned)
            return carry

        lax.fori_loop(0, RECS // 8, eight, 0, unroll=4)
        for s in range(SH):
            both[h, 0:RECS, s * LN : (s + 1) * LN] = tall[pl.ds(s, RECS, stride=8), :].astype(BF16)
        exchange["g", h] = copies.start(both.at[h, 0:RECS], both.at[h, RECS : 2 * RECS], sib)

    def partial(q, c3):
        h, p = q // 3, q % 3
        at = pl.ds(pl.multiple_of(c3 * PLANE, PLANE), PLANE)
        return jnp.dot(
            pick_t[p, at, :], both[h, :, p * PW : (p + 1) * PW], preferred_element_type=F32
        )

    far, near, lines, owns = {}, {}, {}, {}

    def rs1(q):
        a3 = order(q)[2]
        half = PLANE // 2
        far_out[q] = partial(q, place.at(a3, 2)).astype(BF16)
        far[q] = [
            copies.start(far_out.at[q, 0:half, :], far_in.at[q, 0], place.device(a3, 1)),
            copies.start(far_out.at[q, half:PLANE, :], far_in.at[q, 1], place.device(a3, 3)),
        ]

    def rs2(q):
        a3 = order(q)[2]
        half = PLANE // 2
        near[q] = []
        for k, d in enumerate((1, 3)):
            total = partial(q, place.at(a3, d))
            far[q][k].wait_recv()
            more = far_in[q, k].astype(F32)
            halves = [total[0:half], total[half:PLANE]]
            halves[k] = halves[k] + more
            near_out[q, k, 0:half, :] = halves[0].astype(BF16)
            near_out[q, k, half:PLANE, :] = halves[1].astype(BF16)
            near[q].append(copies.start(near_out.at[q, k], near_in.at[q, k], place.device(a3, d)))

    def rs_own(q):
        x[q] = partial(q, place.c[order(q)[2]])

    def line_at(axis, d, size):
        return pl.ds(pl.multiple_of(place.at(axis, d) * size, size), size)

    def rs3(q):
        a2 = order(q)[1]
        arrived(near[q])
        x[q] = x[q] + near_in[q, 0].astype(F32) + near_in[q, 1].astype(F32)
        lines[q] = []
        for k, d in enumerate((1, 3, 2)):
            line_out[q, k] = x[q, line_at(a2, d, LINE), :].astype(BF16)
            lines[q].append(copies.start(line_out.at[q, k], line_in.at[q, k], place.device(a2, d)))

    def rs4(q):
        a1, a2, _ = order(q)
        total = x[q, line_at(a2, 0, LINE), :]
        for k in range(3):
            lines[q][k].wait_recv()
            total = total + line_in[q, k].astype(F32)
        x[q, 0:LINE, :] = total
        owns[q] = []
        for k, d in enumerate((1, 3, 2)):
            own_out[q, k] = x[q, line_at(a1, d, BLK), :].astype(BF16)
            owns[q].append(copies.start(own_out.at[q, k], own_in.at[q, k], place.device(a1, d)))

    def rs5(q):
        total = x[q, line_at(order(q)[0], 0, BLK), :]
        for k in range(3):
            owns[q][k].wait_recv()
            total = total + own_in[q, k].astype(F32)
        for k in range(2):
            gs[pl.ds(q * 2 + k, BLK, stride=16), :] = total[:, k * LN : (k + 1) * LN]

    h0, h1 = (0, 1, 2), (3, 4, 5)
    for q in h0 + h1:
        ag1(q)
    idsb[0] = jnp.zeros((8, RECS), I32)
    idsb[0, 0:1, :] = owner_in[...]
    idsb[0, 1:2, :] = pos_in[...]
    id_copy = copies.start(idsb.at[0], idsb.at[1], sib)
    load_coeffs.wait()
    make_modes()
    make_tables()
    for hq in (h0, h1):
        for q in hq:
            ag2(q)
        for q in hq:
            ag3(q, 0)
    id_copy.wait_recv()
    make_keys()
    make_picks()
    for hq in (h0, h1):
        for d in (3, 1, 2):
            for q in hq:
                ag3(q, d)
    make_picks_t()
    for hq in (h0, h1):
        for d in (0, 3, 1, 2):
            for q in hq:
                ag_forward(q, d)
    gather(0)
    project(0)
    sum1(0)
    gather(1)
    project(1)
    sum2(0)
    sum1(1)
    sum3(0)
    sum2(1)
    weigh(0)
    mix(0)
    sum3(1)
    exchange["g", 0].wait_recv()
    for q in h0:
        rs1(q)
    weigh(1)
    mix(1)
    for q in h0:
        rs2(q)
    exchange["g", 1].wait_recv()
    for q in h1:
        rs1(q)
    for q in h0:
        rs_own(q)
    for q in h0:
        rs3(q)
    for q in h1:
        rs2(q)
    for q in h1:
        rs_own(q)
    for q in h0:
        rs4(q)
    for q in h1:
        rs3(q)
    for r in range(GROUPS):
        corr_out[:, r * MG : (r + 1) * MG] = corr[:, r * MP : r * MP + MG]
    for q in h0:
        rs5(q)
    for q in h1:
        rs4(q)
    for q in h1:
        rs5(q)

    def out_copy(b):
        return pltpu.make_async_copy(gout.at[b], guesses.at[b], osem.at[b])

    def guess(b, carry):
        g = gs[pl.ds(pl.multiple_of(b * 16, 16), S), :]
        comb[0:S, :] = jnp.where(low12, g, -g)
        comb[S : 2 * S, :] = pltpu.roll(g, NB, 1)
        gout[b] = jnp.dot(comb[...].astype(BF16), bbuf[b], preferred_element_type=F32).astype(BF16)
        out_copy(b).start()
        return carry

    lax.fori_loop(0, BLK, guess, 0)
    for b in range(BLK):
        out_copy(b).wait()
    copies.finish()


def shards(basis, sources, old_coeffs, eigenvalues, dest_owner, new_pos):
    hbm = pl.BlockSpec(memory_space=pl.ANY)
    vmem = pl.BlockSpec(memory_space=pltpu.VMEM)
    smem = pl.BlockSpec(memory_space=pltpu.SMEM)
    half_lanes = GROUPS * MP // 2
    guesses, correlations = pl.pallas_call(
        kernel,
        out_shape=(
            jax.ShapeDtypeStruct((BLK, 2 * S, BV), BF16),
            jax.ShapeDtypeStruct((2 * S, MODES), F32),
        ),
        in_specs=[hbm, hbm, hbm, vmem, vmem, smem, vmem],
        out_specs=(hbm, vmem),
        scratch_shapes=[
            pltpu.VMEM((BLK, LN, BV), BF16),
            pltpu.VMEM((BLK, 2 * S, BV), BF16),
            pltpu.VMEM((4 * S, 2 * LN), F32),
            pltpu.VMEM((BLK * 16, LN), F32),
            pltpu.VMEM((2 * S, LN), F32),
            pltpu.VMEM((PARTS, SAME, PW), BF16),
            pltpu.VMEM((2, 8, RECS), I32),
            pltpu.VMEM((RECS // 4, LN), F32),
            pltpu.VMEM((8, GROUPS * MP), F32),
            pltpu.VMEM((RECS // 4 * RR, LN), F32),
            pltpu.VMEM((RECS, MG * LN), BF16),
            pltpu.VMEM((LN, RECS), F32),
            pltpu.VMEM((RECS, LN), F32),
            pltpu.VMEM((3, 2, RECS, SAME), BF16),
            pltpu.VMEM((3, SAME, 2 * RECS), BF16),
            pltpu.VMEM((RECS * MP, LN), F32),
            pltpu.VMEM((RECS * MP, LN), BF16),
            pltpu.VMEM((PARTS, RECS, PW), BF16),
            pltpu.VMEM((PARTS, RECS, PW), BF16),
            pltpu.VMEM((PARTS, RECS, PW), BF16),
            pltpu.VMEM((RECS * RR, LN), F32),
            pltpu.VMEM((H, RR, GROUPS * MP), F32),
            pltpu.VMEM((H, 2, 8, 8, half_lanes), F32),
            pltpu.VMEM((H, 2, 4, 8, half_lanes), F32),
            pltpu.VMEM((H, 2, 2, 4, 8, half_lanes), F32),
            pltpu.VMEM((2 * S, GROUPS * MP), F32),
            pltpu.VMEM((H, GROUPS, RR, LN), BF16),
            pltpu.VMEM((RECS * 8, LN), F32),
            pltpu.VMEM((H, 2 * RECS, HW), BF16),
            pltpu.VMEM((PARTS, PLANE, PW), BF16),
            pltpu.VMEM((PARTS, 2, PLANE // 2, PW), BF16),
            pltpu.VMEM((PARTS, 2, PLANE, PW), BF16),
            pltpu.VMEM((PARTS, 2, PLANE, PW), BF16),
            pltpu.VMEM((PARTS, PLANE, PW), F32),
            pltpu.VMEM((PARTS, 3, LINE, PW), BF16),
            pltpu.VMEM((PARTS, 3, LINE, PW), BF16),
            pltpu.VMEM((PARTS, 3, BLK, PW), BF16),
            pltpu.VMEM((PARTS, 3, BLK, PW), BF16),
            pltpu.VMEM((BLK * 16, LN), F32),
            pltpu.VMEM((2 * S, LN), F32),
            pltpu.VMEM((BLK, 2 * S, BV), BF16),
            pltpu.SemaphoreType.DMA((BLK // 2,)),
            pltpu.SemaphoreType.DMA((BLK // 2,)),
            pltpu.SemaphoreType.DMA((BLK,)),
            pltpu.SemaphoreType.DMA,
            pltpu.SemaphoreType.DMA((N_COPIES,)),
            pltpu.SemaphoreType.DMA((N_COPIES,)),
        ],
        compiler_params=pltpu.CompilerParams(
            collective_id=1, has_side_effects=True, vmem_limit_bytes=60 * MIB
        ),
    )(
        basis, sources, old_coeffs, dest_owner.reshape(1, RECS), new_pos.reshape(1, RECS),
        new_pos, eigenvalues.reshape(1, MODES),
    )
    return guesses.astype(F32), correlations.T


def solution(mesh):
    in_specs = (
        P(("gz", "ta"), None, None),
        P(("gz", "ta"), None, None),
        P(("gz", "ta"), None),
        P(),
        P(("gz", "ta")),
        P(("gz", "ta")),
    )
    out_specs = (P(("gz", "ta"), None, None), P())
    return jax.shard_map(shards, mesh=mesh, in_specs=in_specs, out_specs=out_specs, check_vma=False)
```

time: 163 us -> 98.8 us (0.61)
  Pallas kernels: 0 us -> 92.9 us
  blocking collectives: 63.9 us -> 0 us
  waiting for transfers between devices: 30.1 us -> 0 us
  local copies, waits for them, and re-layouts: 22.8 us -> 0.62 us
  starting transfers between devices: 18.9 us -> 0 us
  matrix products: 18.1 us -> 0 us
  other arithmetic: 7 us -> 4.43 us
    pallas_call x0 -> x1, Pallas kernels: none -> 92.9 us  [shards(): pl.pallas_call(kernel, out_shape=(jax.ShapeDtypeStruct((BLK, 2 * S, BV),...]
    psum x1 -> x0, blocking collectives: 63.9 us -> none  [shards(): proj = lax.psum(partial_correlation, ('gz', 'ta'))]
    all_to_all x2 -> x0, waiting for transfers between devices: 30.1 us -> none  [the longest x1 27.9 us: shards(): lax.all_to_all(outgoing.reshape(device_count, capacity, record_width), ('...]
    all_to_all x2 -> x0, starting transfers between devices: 18.9 us -> none  [the longest x1 11.1 us: shards(): lax.all_to_all(positions.reshape(device_count, capacity), ('gz', 'ta'), s...]
    dot_general x4 -> x0, matrix products: 18.1 us -> none  [the longest x1 8.6 us: shards(): jnp.einsum('bkj,bsj->bks', basis, sources, preferred_element_type=jnp.flo...]
    scatter x3 -> x0, local copies, waits for them, and re-layouts: 13.1 us -> none  [the longest x1 6.73 us: shards(): coeff_table = jnp.zeros((records, record_width), old_coeffs.dtype).at[arr...]
    reshape x4 -> x0, local copies, waits for them, and re-layouts: 6.96 us -> none  [the longest x1 2.45 us: shards(): outgoing.reshape(device_count, capacity, record_width)]
    convert_element_type x1, other arithmetic: 0.12 us -> 4.43 us  [shards(): return (guesses.astype(F32), correlations.T)]
  transfers between devices with their start and end apart: 2 -> 0, of which waited for: 2 -> 0; matrix products, arithmetic and copies ran while one was open for 13% -> 0% of each run, Pallas kernels for 0% -> 0%
where the time goes in v2:
time: 98.8 us; the launch traced here: 98.6 us
  Pallas kernels  92.9 us (94%)
  other arithmetic  4.43 us (4%)
    pallas_call x1, Pallas kernels, shards(): pl.pallas_call(kernel, out_shape=(jax.ShapeDtypeStruct((BLK, 2 * S, BV),...  92.9 us
    convert_element_type x1, other arithmetic, shards(): return (guesses.astype(F32), correlations.T)  4.43 us

profile of v2, /device:TPU:0, one launch (start us, length us, event | category | flops | bytes accessed | tf_op | source)
XLA Modules:
  0.0 98.6 jit_solution(12554162513487909686)
XLA Ops:
  0.6 92.9 %shard_map.77 = (bf16[16,24,3072]{2,1,0:T(8,128)(2,1)}, f32[24,400]{1,0:T(8,128)}) custom-call(bf16[16,128,3072]{2,1,0:T(8,128)(2,1)} %basis.1, bf16[16,24,3072]{2,1,0:T(8,128)(2,1)} %sources.1, bf16[256,3200]{1,0:T(8,128)(2,1)} %coeffs_in.1, s32[1,256]{1,0:T(1,128)} %bitcast.7, s32[1,256]{1,0:T(1,128)} %bitcast.5, s32[256]{0:T(256)} %pos.1, f32[1,400]{1,0:T(1,128)} %bitcast.6), custom_call_target="tpu_custom_call" | custom-call | tf_op jit(solution)/shard_map/pallas_call | solution.py:571
  93.6 0.0 copy-start
  93.6 4.4 %convert_element_type.3 = f32[16,24,3072]{2,1,0:T(8,128)} convert(bf16[16,24,3072]{2,1,0:T(8,128)(2,1)} %get-tuple-element.4) | non-fusion elementwise | flops 1179648 | bytes 7077888 | tf_op jit(solution)/shard_map/convert_element_type | solution.py:635
  98.0 0.0 copy-done
  98.0 0.6 copy.9
Async XLA Ops:
  93.6 4.4 %copy-start = (f32[24,400]{1,0:T(8,128)S(1)}, f32[24,400]{1,0:T(8,128)}, u32[]{:S(2)}) copy-start(f32[24,400]{1,0:T(8,128)} %get-tuple-element.5) | copy-start | bytes 115204

commit v3 on v2

--- a/solution.py
+++ b/solution.py
@@ -29,7 +29,7 @@
 SAME = 64 * BLK
 PLANE, LINE = 16 * BLK, 4 * BLK
 MIB = 1 << 20
-N_COPIES = 1 + PARTS * 22 + PARTS + H * (14 + 6 + 14) + H + PARTS * 10
+N_COPIES = 1 + PARTS * 22 + PARTS + H * (14 + 6 + 14) + H + PARTS * 18
 
 
 class Place:
@@ -38,13 +38,19 @@
         ta = lax.axis_index("ta")
         self.core = lax.rem(gz, 2)
         self.c = (ta // 4, gz // 2, lax.rem(ta, 4))
+        self.known = {}
 
     def at(self, axis, d):
-        return lax.rem(self.c[axis] + d, 4)
+        if (axis, d) not in self.known:
+            self.known[axis, d] = lax.rem(self.c[axis] + d, 4) if d else self.c[axis]
+        return self.known[axis, d]
 
     def device(self, axis, d, flip=False):
-        x, y, z = (self.at(a, d) if a == axis else self.c[a] for a in range(3))
-        return (y * 2 + (1 - self.core if flip else self.core), x * 4 + z)
+        if (axis, d, flip) not in self.known:
+            x, y, z = (self.at(a, d) if a == axis else self.c[a] for a in range(3))
+            core = 1 - self.core if flip else self.core
+            self.known[axis, d, flip] = (y * 2 + core, x * 4 + z)
+        return self.known[axis, d, flip]
 
 
 def order(q):
@@ -53,7 +59,7 @@
 
 class Copies:
     def __init__(self, send, recv):
-        self.send, self.recv, self.all = send, recv, []
+        self.send, self.recv, self.all, self.settled = send, recv, [], 0
 
     def start(self, src, dst, device):
         n = len(self.all)
@@ -69,9 +75,11 @@
         self.all.append(copy)
         return copy
 
-    def finish(self):
-        for copy in self.all:
+    def settle(self, until=None):
+        until = len(self.all) if until is None else until
+        for copy in self.all[self.settled : until]:
             copy.wait_send()
+        self.settled = until
 
 
 def arrived(copies):
@@ -94,11 +102,11 @@
 
 def kernel(
     basis, sources, coeffs_in, owner_in, pos_in, pos, eig_in,
-    guesses, corr_out,
-    bbuf, sbuf, prod, stage, sq, table, idsb, lane_group, eig, terms, coeffs, kbig, kcol, pick, pick_t, wide, modes,
+    g_out, corr_out, bbuf,
+    sbuf, prod, stage, sq, table, idsb, lane_group, eig, terms, coeffs, kbig, kcol, pick, pick_t, wide, modes,
     mine, theirs, got, xs, pay, ar1, ar2, ar3, corr, wt, tall, both,
-    far_out, far_in, near_out, near_in, x, line_out, line_in, own_out, own_in, gs, comb, gout,
-    bsem, ssem, osem, csem, send, recv,
+    far_out, far_in, near_sum, near_out, near_in, x, line_out, line_in, own_out, own_in, gs,
+    bsem, ssem, csem, send, recv,
 ):
     place = Place()
     core = place.core
@@ -217,7 +225,7 @@
         for who in range(2):
             for p in range(3):
                 k = who * 3 + p
-                pick[p, who] = jnp.where(kcol[:, k : k + 1] == wide_ids, 1.0, 0.0).astype(BF16)
+                pick[p, (1 - who) * RECS : (2 - who) * RECS, :] = jnp.where(kcol[:, k : k + 1] == wide_ids, 1.0, 0.0).astype(BF16)
 
     def make_picks_t():
         tall_ids = iota((SAME, RECS), 0).astype(F32)
@@ -259,16 +267,15 @@
             q = h * 3 + p
             for d in range(4):
                 arrived(last[q, d])
-            theirs[q] = jnp.dot(pick[p, 1], table[q], preferred_element_type=F32).astype(BF16)
+            found = jnp.dot(pick[p], table[q], preferred_element_type=F32)
+            theirs[q] = found[0:RECS].astype(BF16)
             exchange[q] = copies.start(theirs.at[q], got.at[q], sib)
-        for p in range(3):
-            q = h * 3 + p
-            mine[q] = jnp.dot(pick[p, 0], table[q], preferred_element_type=F32).astype(BF16)
+            mine[q] = found[RECS : 2 * RECS].astype(BF16)
 
     low_rec = low_lanes((RECS, LN))
     group32 = iota((RR, LN), 1) // MP
 
-    def project(h):
+    def project_start(h):
         for s in (6, 7, 14, 15):
             xs[pl.ds(s, RECS, stride=RR), :] = jnp.zeros((RECS, LN), F32)
         for p in range(3):
@@ -281,6 +288,7 @@
                 xs[pl.ds(2 * p + k, RECS, stride=RR), :] = real
                 xs[pl.ds(8 + 2 * p + k, RECS, stride=RR), :] = jnp.where(low_rec, turned, -turned)
 
+    def project(h):
         def eight(g, carry):
             left = xs[pl.ds(pl.multiple_of(g * 8 * RR, 8 * RR), 8 * RR), :].astype(BF16)
             right = modes[pl.ds(pl.multiple_of(g * 8 * MP, 8 * MP), 8 * MP), :]
@@ -294,7 +302,7 @@
                 terms[pl.ds(pl.multiple_of((g * 2 + t) * RR, RR), RR), :] = term
             return carry
 
-        lax.fori_loop(0, RECS // 8, eight, 0, unroll=4)
+        lax.fori_loop(0, RECS // 8, eight, 0, unroll=8)
 
         def four(g, acc):
             term = terms[pl.ds(pl.multiple_of(g * RR, RR), RR), :]
@@ -404,7 +412,7 @@
                 tall[at, :] = real + jnp.where(low8, -turned, turned)
             return carry
 
-        lax.fori_loop(0, RECS // 8, eight, 0, unroll=4)
+        lax.fori_loop(0, RECS // 8, eight, 0, unroll=8)
         for s in range(SH):
             both[h, 0:RECS, s * LN : (s + 1) * LN] = tall[pl.ds(s, RECS, stride=8), :].astype(BF16)
         exchange["g", h] = copies.start(both.at[h, 0:RECS], both.at[h, RECS : 2 * RECS], sib)
@@ -418,50 +426,71 @@
 
     far, near, lines, owns = {}, {}, {}, {}
 
+    by_side = ((2, 1), (3, 0))
+
+    def line_at(axis, d, size):
+        return pl.ds(pl.multiple_of(place.at(axis, d) * size, size), size)
+
     def rs1(q):
-        a3 = order(q)[2]
-        half = PLANE // 2
+        _, a2, a3 = order(q)
         far_out[q] = partial(q, place.at(a3, 2)).astype(BF16)
-        far[q] = [
-            copies.start(far_out.at[q, 0:half, :], far_in.at[q, 0], place.device(a3, 1)),
-            copies.start(far_out.at[q, half:PLANE, :], far_in.at[q, 1], place.device(a3, 3)),
-        ]
+        for k, d in enumerate((1, 3)):
+            for j, n in enumerate(by_side[k]):
+                far[q, k, j] = copies.start(
+                    far_out.at[q, line_at(a2, n, LINE), :], far_in.at[q, k, j], place.device(a3, d)
+                )
+
+    def send_near(q, k, n):
+        _, a2, a3 = order(q)
+        near[q, k, n] = copies.start(
+            near_out.at[q, k, line_at(a2, n, LINE), :],
+            near_in.at[q, k, n],
+            place.device(a3, (1, 3)[k]),
+        )
+
+    def rs_near(q):
+        _, a2, a3 = order(q)
+        for k, d in enumerate((1, 3)):
+            near_sum[q, k] = partial(q, place.at(a3, d))
+            for n in by_side[1 - k]:
+                at = line_at(a2, n, LINE)
+                near_out[q, k, at, :] = near_sum[q, k, at, :].astype(BF16)
+                send_near(q, k, n)
 
     def rs2(q):
-        a3 = order(q)[2]
-        half = PLANE // 2
-        near[q] = []
-        for k, d in enumerate((1, 3)):
-            total = partial(q, place.at(a3, d))
-            far[q][k].wait_recv()
-            more = far_in[q, k].astype(F32)
-            halves = [total[0:half], total[half:PLANE]]
-            halves[k] = halves[k] + more
-            near_out[q, k, 0:half, :] = halves[0].astype(BF16)
-            near_out[q, k, half:PLANE, :] = halves[1].astype(BF16)
-            near[q].append(copies.start(near_out.at[q, k], near_in.at[q, k], place.device(a3, d)))
+        a2 = order(q)[1]
+        for k in range(2):
+            for j, n in enumerate(by_side[k]):
+                far[q, k, j].wait_recv()
+                at = line_at(a2, n, LINE)
+                total = near_sum[q, k, at, :] + far_in[q, k, j].astype(F32)
+                near_out[q, k, at, :] = total.astype(BF16)
+                send_near(q, k, n)
 
     def rs_own(q):
         x[q] = partial(q, place.c[order(q)[2]])
 
-    def line_at(axis, d, size):
-        return pl.ds(pl.multiple_of(place.at(axis, d) * size, size), size)
+    def whole_line(q, n):
+        total = x[q, line_at(order(q)[1], n, LINE), :]
+        for k in range(2):
+            near[q, k, n].wait_recv()
+            total = total + near_in[q, k, n].astype(F32)
+        return total
 
     def rs3(q):
         a2 = order(q)[1]
-        arrived(near[q])
-        x[q] = x[q] + near_in[q, 0].astype(F32) + near_in[q, 1].astype(F32)
-        lines[q] = []
-        for k, d in enumerate((1, 3, 2)):
-            line_out[q, k] = x[q, line_at(a2, d, LINE), :].astype(BF16)
-            lines[q].append(copies.start(line_out.at[q, k], line_in.at[q, k], place.device(a2, d)))
+        for n in (2, 1, 3):
+            line_out[q, n - 1] = whole_line(q, n).astype(BF16)
+            lines[q, n] = copies.start(
+                line_out.at[q, n - 1], line_in.at[q, n - 1], place.device(a2, n)
+            )
 
     def rs4(q):
-        a1, a2, _ = order(q)
-        total = x[q, line_at(a2, 0, LINE), :]
-        for k in range(3):
-            lines[q][k].wait_recv()
-            total = total + line_in[q, k].astype(F32)
+        a1 = order(q)[0]
+        total = whole_line(q, 0)
+        for n in (1, 3, 2):
+            lines[q, n].wait_recv()
+            total = total + line_in[q, n - 1].astype(F32)
         x[q, 0:LINE, :] = total
         owns[q] = []
         for k, d in enumerate((1, 3, 2)):
@@ -499,25 +528,37 @@
             for q in hq:
                 ag3(q, d)
     make_picks_t()
-    for hq in (h0, h1):
-        for d in (0, 3, 1, 2):
-            for q in hq:
-                ag_forward(q, d)
+    for d in (0, 3, 1, 2):
+        for q in h0:
+            ag_forward(q, d)
+    for q in h1:
+        ag_forward(q, 0)
     gather(0)
+    for d in (3, 1):
+        for q in h1:
+            ag_forward(q, d)
+    project_start(0)
+    for q in h1:
+        ag_forward(q, 2)
     project(0)
     sum1(0)
     gather(1)
+    project_start(1)
     project(1)
+    sum1(1)
     sum2(0)
-    sum1(1)
     sum3(0)
     sum2(1)
+    sum3(1)
     weigh(0)
     mix(0)
-    sum3(1)
     exchange["g", 0].wait_recv()
     for q in h0:
         rs1(q)
+    for q in h0:
+        rs_near(q)
+    for q in h0:
+        rs_own(q)
     weigh(1)
     mix(1)
     for q in h0:
@@ -525,42 +566,56 @@
     exchange["g", 1].wait_recv()
     for q in h1:
         rs1(q)
-    for q in h0:
+    for q in h1:
+        rs_near(q)
+    for q in h1:
         rs_own(q)
-    for q in h0:
-        rs3(q)
+    far_sent = len(copies.all)
     for q in h1:
         rs2(q)
-    for q in h1:
-        rs_own(q)
+    copies.settle(far_sent)
     for q in h0:
-        rs4(q)
-    for q in h1:
         rs3(q)
     for r in range(GROUPS):
         corr_out[:, r * MG : (r + 1) * MG] = corr[:, r * MP : r * MP + MG]
+    for q in h1:
+        rs3(q)
     for q in h0:
-        rs5(q)
+        rs4(q)
+    copies.settle()
     for q in h1:
         rs4(q)
-    for q in h1:
+    for q in h0 + h1:
         rs5(q)
-
-    def out_copy(b):
-        return pltpu.make_async_copy(gout.at[b], guesses.at[b], osem.at[b])
-
-    def guess(b, carry):
-        g = gs[pl.ds(pl.multiple_of(b * 16, 16), S), :]
-        comb[0:S, :] = jnp.where(low12, g, -g)
-        comb[S : 2 * S, :] = pltpu.roll(g, NB, 1)
-        gout[b] = jnp.dot(comb[...].astype(BF16), bbuf[b], preferred_element_type=F32).astype(BF16)
-        out_copy(b).start()
+    g_out[...] = gs[...]
+    copies.settle()
+
+
+def guess_kernel(g_in, corr_in, bbuf, guesses, corr_out, comb, gout, osem):
+    corr_out[...] = corr_in[...]
+    low12 = low_lanes((S, LN))
+
+    def out_copy(j):
+        at = pl.ds(j * 2, 2)
+        return pltpu.make_async_copy(gout.at[at], guesses.at[at], osem.at[j])
+
+    def guess(j, carry):
+        for k in range(2):
+            g = g_in[pl.ds(pl.multiple_of((j * 2 + k) * 16, 16), S), :]
+            lanes = slice(k * LN, (k + 1) * LN)
+            comb[2 * S * k : 2 * S * k + S, lanes] = jnp.where(low12, g, -g)
+            comb[2 * S * k + S : 2 * S * (k + 1), lanes] = pltpu.roll(g, NB, 1)
+        vectors = bbuf[pl.ds(j * 2, 2)].reshape(2 * LN, BV)
+        out = jnp.dot(comb[...].astype(BF16), vectors, preferred_element_type=F32)
+        gout[j * 2] = out[0 : 2 * S]
+        gout[j * 2 + 1] = out[2 * S : 4 * S]
+        out_copy(j).start()
         return carry
 
-    lax.fori_loop(0, BLK, guess, 0)
-    for b in range(BLK):
-        out_copy(b).wait()
-    copies.finish()
+    comb[...] = jnp.zeros_like(comb)
+    lax.fori_loop(0, BLK // 2, guess, 0, unroll=2)
+    for j in range(BLK // 2):
+        out_copy(j).wait()
 
 
 def shards(basis, sources, old_coeffs, eigenvalues, dest_owner, new_pos):
@@ -568,16 +623,16 @@
     vmem = pl.BlockSpec(memory_space=pltpu.VMEM)
     smem = pl.BlockSpec(memory_space=pltpu.SMEM)
     half_lanes = GROUPS * MP // 2
-    guesses, correlations = pl.pallas_call(
+    g, corr, vectors = pl.pallas_call(
         kernel,
         out_shape=(
-            jax.ShapeDtypeStruct((BLK, 2 * S, BV), BF16),
-            jax.ShapeDtypeStruct((2 * S, MODES), F32),
+            pltpu.VMEM((BLK * 16, LN), F32),
+            pltpu.VMEM((2 * S, MODES), F32),
+            pltpu.VMEM((BLK, LN, BV), BF16),
         ),
         in_specs=[hbm, hbm, hbm, vmem, vmem, smem, vmem],
-        out_specs=(hbm, vmem),
+        out_specs=(vmem, vmem, vmem),
         scratch_shapes=[
-            pltpu.VMEM((BLK, LN, BV), BF16),
             pltpu.VMEM((BLK, 2 * S, BV), BF16),
             pltpu.VMEM((4 * S, 2 * LN), F32),
             pltpu.VMEM((BLK * 16, LN), F32),
@@ -590,7 +645,7 @@
             pltpu.VMEM((RECS, MG * LN), BF16),
             pltpu.VMEM((LN, RECS), F32),
             pltpu.VMEM((RECS, LN), F32),
-            pltpu.VMEM((3, 2, RECS, SAME), BF16),
+            pltpu.VMEM((3, 2 * RECS, SAME), BF16),
             pltpu.VMEM((3, SAME, 2 * RECS), BF16),
             pltpu.VMEM((RECS * MP, LN), F32),
             pltpu.VMEM((RECS * MP, LN), BF16),
@@ -607,32 +662,45 @@
             pltpu.VMEM((RECS * 8, LN), F32),
             pltpu.VMEM((H, 2 * RECS, HW), BF16),
             pltpu.VMEM((PARTS, PLANE, PW), BF16),
-            pltpu.VMEM((PARTS, 2, PLANE // 2, PW), BF16),
+            pltpu.VMEM((PARTS, 2, 2, LINE, PW), BF16),
+            pltpu.VMEM((PARTS, 2, PLANE, PW), F32),
             pltpu.VMEM((PARTS, 2, PLANE, PW), BF16),
-            pltpu.VMEM((PARTS, 2, PLANE, PW), BF16),
+            pltpu.VMEM((PARTS, 2, 4, LINE, PW), BF16),
             pltpu.VMEM((PARTS, PLANE, PW), F32),
             pltpu.VMEM((PARTS, 3, LINE, PW), BF16),
             pltpu.VMEM((PARTS, 3, LINE, PW), BF16),
             pltpu.VMEM((PARTS, 3, BLK, PW), BF16),
             pltpu.VMEM((PARTS, 3, BLK, PW), BF16),
             pltpu.VMEM((BLK * 16, LN), F32),
-            pltpu.VMEM((2 * S, LN), F32),
-            pltpu.VMEM((BLK, 2 * S, BV), BF16),
             pltpu.SemaphoreType.DMA((BLK // 2,)),
             pltpu.SemaphoreType.DMA((BLK // 2,)),
-            pltpu.SemaphoreType.DMA((BLK,)),
             pltpu.SemaphoreType.DMA,
             pltpu.SemaphoreType.DMA((N_COPIES,)),
             pltpu.SemaphoreType.DMA((N_COPIES,)),
         ],
         compiler_params=pltpu.CompilerParams(
-            collective_id=1, has_side_effects=True, vmem_limit_bytes=60 * MIB
+            collective_id=1, has_side_effects=True, vmem_limit_bytes=46 * MIB
         ),
     )(
         basis, sources, old_coeffs, dest_owner.reshape(1, RECS), new_pos.reshape(1, RECS),
         new_pos, eigenvalues.reshape(1, MODES),
     )
-    return guesses.astype(F32), correlations.T
+    guesses, correlations = pl.pallas_call(
+        guess_kernel,
+        out_shape=(
+            jax.ShapeDtypeStruct((BLK, 2 * S, BV), F32),
+            jax.ShapeDtypeStruct((2 * S, MODES), F32),
+        ),
+        in_specs=[vmem, vmem, vmem],
+        out_specs=(hbm, vmem),
+        scratch_shapes=[
+            pltpu.VMEM((4 * S, 2 * LN), F32),
+            pltpu.VMEM((BLK, 2 * S, BV), F32),
+            pltpu.SemaphoreType.DMA((BLK // 2,)),
+        ],
+        compiler_params=pltpu.CompilerParams(vmem_limit_bytes=16 * MIB),
+    )(g, corr, vectors)
+    return guesses, correlations.T
 
 
 def solution(mesh):

time: 98.8 us -> 87.7 us (0.89)
  Pallas kernels: 92.9 us -> 86.8 us
  other arithmetic: 4.43 us -> 0 us
    pallas_call x1 -> x2, Pallas kernels: 92.9 us -> 86.8 us  [the longest x1 82.4 us: shards(): pl.pallas_call(kernel, out_shape=(pltpu.VMEM((BLK * 16, LN), F32), pltpu....]
    convert_element_type x1 -> x0, other arithmetic: 4.43 us -> none  [shards(): return (guesses.astype(F32), correlations.T)]
where the time goes in v3:
time: 87.7 us; the launch traced here: 87.6 us
  Pallas kernels  86.8 us (99%)
    pallas_call x1, Pallas kernels, shards(): pl.pallas_call(kernel, out_shape=(pltpu.VMEM((BLK * 16, LN), F32), pltpu....  82.4 us
    pallas_call x1, Pallas kernels, shards(): pl.pallas_call(guess_kernel, out_shape=(jax.ShapeDtypeStruct((BLK, 2 * S,...  4.33 us

profile of v3, /device:TPU:0, one launch (start us, length us, event | category | flops | bytes accessed | tf_op | source)
XLA Modules:
  0.0 87.6 jit_solution(3043655895396359614)
XLA Ops:
  0.6 82.4 %shard_map.77 = (f32[256,128]{1,0:T(8,128)S(1)}, f32[24,400]{1,0:T(8,128)S(1)}, bf16[16,128,3072]{2,1,0:T(8,128)(2,1)S(1)}) custom-call(bf16[16,128,3072]{2,1,0:T(8,128)(2,1)} %basis.1, bf16[16,24,3072]{2,1,0:T(8,128)(2,1)} %sources.1, bf16[256,3200]{1,0:T(8,128)(2,1)} %coeffs_in.1, s32[1,256]{1,0:T(1,128)} %bitcast.6, s32[1,256]{1,0:T(1,128)} %bitcast.4, ...), custom_call_target="tpu_custom_call" | custom-call | tf_op jit(solution)/shard_map/pallas_call | solution.py:626
  83.1 4.3 %shard_map.78 = (f32[16,24,3072]{2,1,0:T(8,128)}, f32[24,400]{1,0:T(8,128)}) custom-call(f32[256,128]{1,0:T(8,128)S(1)} %get-tuple-element.7.g_in, f32[24,400]{1,0:T(8,128)S(1)} %get-tuple-element.8.corr_in, bf16[16,128,3072]{2,1,0:T(8,128)(2,1)S(1)} %get-tuple-element.9.bbuf), custom_call_target="tpu_custom_call" | custom-call | tf_op jit(solution)/shard_map/pallas_call | solution.py:688

commit v4 on v3

--- a/solution.py
+++ b/solution.py
@@ -29,7 +29,7 @@
 SAME = 64 * BLK
 PLANE, LINE = 16 * BLK, 4 * BLK
 MIB = 1 << 20
-N_COPIES = 1 + PARTS * 22 + PARTS + H * (14 + 6 + 14) + H + PARTS * 18
+N_COPIES = 1 + PARTS * 22 + PARTS + H * (14 + 6 + 14) + 2 * H + PARTS * 18
 
 
 class Place:
@@ -101,12 +101,12 @@
 
 
 def kernel(
-    basis, sources, coeffs_in, owner_in, pos_in, pos, eig_in,
+    basis, sources, coeffs_in, owner_hbm, pos_hbm, pos_flat, eig_hbm,
     g_out, corr_out, bbuf,
-    sbuf, prod, stage, sq, table, idsb, lane_group, eig, terms, coeffs, kbig, kcol, pick, pick_t, wide, modes,
+    owner_in, pos_in, pos, eig_in, sbuf, prod, stage, sq, table, idsb, lane_group, eig, terms, coeffs, kbig, kcol, pick, pick_t, wide, modes,
     mine, theirs, got, xs, pay, ar1, ar2, ar3, corr, wt, tall, both,
     far_out, far_in, near_sum, near_out, near_in, x, line_out, line_in, own_out, own_in, gs,
-    bsem, ssem, csem, send, recv,
+    bsem, ssem, csem, isem, send, recv,
 ):
     place = Place()
     core = place.core
@@ -125,6 +125,14 @@
             copy.start()
     load_coeffs = pltpu.make_async_copy(coeffs_in, coeffs, csem)
     load_coeffs.start()
+    small_loads = [
+        pltpu.make_async_copy(src, dst, isem.at[k])
+        for k, (src, dst) in enumerate(
+            ((owner_hbm, owner_in), (pos_hbm, pos_in), (pos_flat, pos), (eig_hbm, eig_in))
+        )
+    ]
+    for copy in small_loads:
+        copy.start()
     barrier = pltpu.get_barrier_semaphore()
     friends = [sib] + [place.device(a, d, f) for a in range(3) for d in (1, 2, 3) for f in (False, True)]
     for friend in friends:
@@ -159,9 +167,6 @@
         return total
 
     total = lax.fori_loop(0, BLK // 2, block_pair, jnp.zeros((4 * S, LN), F32))
-    sq[...] = jnp.broadcast_to(
-        jnp.sum(total[0 : 2 * S] + total[2 * S : 4 * S], axis=1, keepdims=True), (2 * S, LN)
-    )
     pl.semaphore_wait(barrier, len(friends))
 
     def row(c3, c2, c1=0):
@@ -267,17 +272,18 @@
             q = h * 3 + p
             for d in range(4):
                 arrived(last[q, d])
-            found = jnp.dot(pick[p], table[q], preferred_element_type=F32)
-            theirs[q] = found[0:RECS].astype(BF16)
+            found = jnp.dot(pick[p, 0:RECS], table[q], preferred_element_type=F32)
+            theirs[q] = found.astype(BF16)
             exchange[q] = copies.start(theirs.at[q], got.at[q], sib)
-            mine[q] = found[RECS : 2 * RECS].astype(BF16)
+        for p in range(3):
+            q = h * 3 + p
+            found = jnp.dot(pick[p, RECS : 2 * RECS], table[q], preferred_element_type=F32)
+            mine[q] = found.astype(BF16)
 
     low_rec = low_lanes((RECS, LN))
     group32 = iota((RR, LN), 1) // MP
 
     def project_start(h):
-        for s in (6, 7, 14, 15):
-            xs[pl.ds(s, RECS, stride=RR), :] = jnp.zeros((RECS, LN), F32)
         for p in range(3):
             q = h * 3 + p
             exchange[q].wait_recv()
@@ -412,10 +418,16 @@
                 tall[at, :] = real + jnp.where(low8, -turned, turned)
             return carry
 
-        lax.fori_loop(0, RECS // 8, eight, 0, unroll=8)
-        for s in range(SH):
-            both[h, 0:RECS, s * LN : (s + 1) * LN] = tall[pl.ds(s, RECS, stride=8), :].astype(BF16)
-        exchange["g", h] = copies.start(both.at[h, 0:RECS], both.at[h, RECS : 2 * RECS], sib)
+        half = RECS // 2
+        exchange["g", h] = []
+        for k in range(2):
+            lax.fori_loop(k * half // 8, (k + 1) * half // 8, eight, 0, unroll=8)
+            ours = slice(k * half, (k + 1) * half)
+            for s in range(SH):
+                part = tall[pl.ds(k * half * 8 + s, half, stride=8), :]
+                both[h, ours, s * LN : (s + 1) * LN] = part.astype(BF16)
+            away = both.at[h, RECS + k * half : RECS + (k + 1) * half]
+            exchange["g", h].append(copies.start(both.at[h, ours], away, sib))
 
     def partial(q, c3):
         h, p = q // 3, q % 3
@@ -508,6 +520,11 @@
     h0, h1 = (0, 1, 2), (3, 4, 5)
     for q in h0 + h1:
         ag1(q)
+    sq[...] = jnp.broadcast_to(
+        jnp.sum(total[0 : 2 * S] + total[2 * S : 4 * S], axis=1, keepdims=True), (2 * S, LN)
+    )
+    for copy in small_loads:
+        copy.wait()
     idsb[0] = jnp.zeros((8, RECS), I32)
     idsb[0, 0:1, :] = owner_in[...]
     idsb[0, 1:2, :] = pos_in[...]
@@ -515,6 +532,8 @@
     load_coeffs.wait()
     make_modes()
     make_tables()
+    for s in (6, 7, 14, 15):
+        xs[pl.ds(s, RECS, stride=RR), :] = jnp.zeros((RECS, LN), F32)
     for hq in (h0, h1):
         for q in hq:
             ag2(q)
@@ -544,38 +563,36 @@
     sum1(0)
     gather(1)
     project_start(1)
+    sum2(0)
     project(1)
     sum1(1)
-    sum2(0)
     sum3(0)
     sum2(1)
-    sum3(1)
     weigh(0)
     mix(0)
-    exchange["g", 0].wait_recv()
+    sum3(1)
+    arrived(exchange["g", 0])
     for q in h0:
         rs1(q)
     for q in h0:
         rs_near(q)
-    for q in h0:
-        rs_own(q)
     weigh(1)
     mix(1)
     for q in h0:
         rs2(q)
-    exchange["g", 1].wait_recv()
+    arrived(exchange["g", 1])
     for q in h1:
         rs1(q)
     for q in h1:
         rs_near(q)
-    for q in h1:
+    for q in h0 + h1:
         rs_own(q)
+    for q in h0:
+        rs3(q)
     far_sent = len(copies.all)
     for q in h1:
         rs2(q)
     copies.settle(far_sent)
-    for q in h0:
-        rs3(q)
     for r in range(GROUPS):
         corr_out[:, r * MG : (r + 1) * MG] = corr[:, r * MP : r * MP + MG]
     for q in h1:
@@ -613,7 +630,7 @@
         return carry
 
     comb[...] = jnp.zeros_like(comb)
-    lax.fori_loop(0, BLK // 2, guess, 0, unroll=2)
+    lax.fori_loop(0, BLK // 2, guess, 0, unroll=8)
     for j in range(BLK // 2):
         out_copy(j).wait()
 
@@ -621,7 +638,6 @@
 def shards(basis, sources, old_coeffs, eigenvalues, dest_owner, new_pos):
     hbm = pl.BlockSpec(memory_space=pl.ANY)
     vmem = pl.BlockSpec(memory_space=pltpu.VMEM)
-    smem = pl.BlockSpec(memory_space=pltpu.SMEM)
     half_lanes = GROUPS * MP // 2
     g, corr, vectors = pl.pallas_call(
         kernel,
@@ -630,9 +646,13 @@
             pltpu.VMEM((2 * S, MODES), F32),
             pltpu.VMEM((BLK, LN, BV), BF16),
         ),
-        in_specs=[hbm, hbm, hbm, vmem, vmem, smem, vmem],
+        in_specs=[hbm] * 7,
         out_specs=(vmem, vmem, vmem),
         scratch_shapes=[
+            pltpu.VMEM((1, RECS), I32),
+            pltpu.VMEM((1, RECS), I32),
+            pltpu.SMEM((RECS,), I32),
+            pltpu.VMEM((1, MODES), F32),
             pltpu.VMEM((BLK, 2 * S, BV), BF16),
             pltpu.VMEM((4 * S, 2 * LN), F32),
             pltpu.VMEM((BLK * 16, LN), F32),
@@ -675,6 +695,7 @@
             pltpu.SemaphoreType.DMA((BLK // 2,)),
             pltpu.SemaphoreType.DMA((BLK // 2,)),
             pltpu.SemaphoreType.DMA,
+            pltpu.SemaphoreType.DMA((4,)),
             pltpu.SemaphoreType.DMA((N_COPIES,)),
             pltpu.SemaphoreType.DMA((N_COPIES,)),
         ],

time: 87.7 us -> 82.8 us (0.944)
  Pallas kernels: 86.8 us -> 81.9 us
    pallas_call x1, Pallas kernels: 82.4 us -> 78 us  [shards(): pl.pallas_call(kernel, out_shape=(pltpu.VMEM((BLK * 16, LN), F32), pltpu....]
where the time goes in v4:
time: 82.8 us; the launch traced here: 82.7 us
  Pallas kernels  81.9 us (99%)
    pallas_call x1, Pallas kernels, shards(): pl.pallas_call(kernel, out_shape=(pltpu.VMEM((BLK * 16, LN), F32), pltpu....  78 us
    pallas_call x1, Pallas kernels, shards(): pl.pallas_call(guess_kernel, out_shape=(jax.ShapeDtypeStruct((BLK, 2 * S,...  3.86 us

profile of v4, /device:TPU:0, one launch (start us, length us, event | category | flops | bytes accessed | tf_op | source)
XLA Modules:
  0.0 82.7 jit_solution(13752076820190355623)
XLA Ops:
  0.6 78.0 %shard_map.77 = (f32[256,128]{1,0:T(8,128)S(1)}, f32[24,400]{1,0:T(8,128)S(1)}, bf16[16,128,3072]{2,1,0:T(8,128)(2,1)S(1)}) custom-call(bf16[16,128,3072]{2,1,0:T(8,128)(2,1)} %basis.1, bf16[16,24,3072]{2,1,0:T(8,128)(2,1)} %sources.1, bf16[256,3200]{1,0:T(8,128)(2,1)} %coeffs_in.1, s32[1,256]{1,0:T(1,128)} %bitcast.6, s32[1,256]{1,0:T(1,128)} %bitcast.4, ...), custom_call_target="tpu_custom_call" | custom-call | tf_op jit(solution)/shard_map/pallas_call | solution.py:642
  78.6 3.9 %shard_map.78 = (f32[16,24,3072]{2,1,0:T(8,128)}, f32[24,400]{1,0:T(8,128)}) custom-call(f32[256,128]{1,0:T(8,128)S(1)} %get-tuple-element.7.g_in, f32[24,400]{1,0:T(8,128)S(1)} %get-tuple-element.8.corr_in, bf16[16,128,3072]{2,1,0:T(8,128)(2,1)S(1)} %get-tuple-element.9.bbuf), custom_call_target="tpu_custom_call" | custom-call | tf_op jit(solution)/shard_map/pallas_call | solution.py:709

commit v5 on v4

--- a/solution.py
+++ b/solution.py
@@ -187,7 +187,7 @@
         s = q * 2
         own = [stage[pl.ds(s + k, BLK, stride=16), :] for k in range(2)]
         table[q, pl.ds(here, BLK), :] = jnp.concatenate(own, axis=1).astype(BF16)
-        first[q] = to_axis(q, a1, here, BLK, (1, 3, 2))
+        first[q] = to_axis(q, a1, here, BLK, (2, 1, 3))
 
     def ag2(q):
         _, a2, a3 = order(q)
@@ -344,7 +344,7 @@
             dst = ar1.at[h, v, slot]
             steps[1, h, v] = [
                 copies.start(pay.at[h, piece, other if f else ours], dst, place.device(axis, d, f))
-                for d in (0, 1, 3, 2) for f in (False, True) if d or f
+                for d in (2, 1, 3, 0) for f in (False, True) if d or f
             ]
 
     def sum2(h):
@@ -357,7 +357,7 @@
             slot = place.c[axis]
             ar2[h, v, slot] = total
             ref = ar2.at[h, v, slot]
-            steps[2, h, v] = [copies.start(ref, ref, place.device(axis, d)) for d in (1, 3, 2)]
+            steps[2, h, v] = [copies.start(ref, ref, place.device(axis, d)) for d in (2, 1, 3)]
 
     def sum3(h):
         for v in range(2):
@@ -369,7 +369,7 @@
             ref = ar3.at[h, v, core, slot]
             steps[3, h, v] = [
                 copies.start(ref, ref, place.device(axis, d, f))
-                for d in (0, 1, 3, 2) for f in (False, True) if d or f
+                for d in (2, 1, 3, 0) for f in (False, True) if d or f
             ]
 
     def weigh(h):
@@ -505,7 +505,7 @@
             total = total + line_in[q, n - 1].astype(F32)
         x[q, 0:LINE, :] = total
         owns[q] = []
-        for k, d in enumerate((1, 3, 2)):
+        for k, d in enumerate((2, 1, 3)):
             own_out[q, k] = x[q, line_at(a1, d, BLK), :].astype(BF16)
             owns[q].append(copies.start(own_out.at[q, k], own_in.at[q, k], place.device(a1, d)))
 
@@ -550,15 +550,11 @@
     for d in (0, 3, 1, 2):
         for q in h0:
             ag_forward(q, d)
-    for q in h1:
-        ag_forward(q, 0)
-    gather(0)
-    for d in (3, 1):
+    for d in (0, 3, 1, 2):
         for q in h1:
             ag_forward(q, d)
+    gather(0)
     project_start(0)
-    for q in h1:
-        ag_forward(q, 2)
     project(0)
     sum1(0)
     gather(1)

time: 82.8 us -> 82.3 us (level)
  no operation moved by 1% of the time
where the time goes in v5:
time: 82.3 us; the launch traced here: 82.1 us
  Pallas kernels  81.3 us (99%)
    pallas_call x1, Pallas kernels, shards(): pl.pallas_call(kernel, out_shape=(pltpu.VMEM((BLK * 16, LN), F32), pltpu....  77.5 us
    pallas_call x1, Pallas kernels, shards(): pl.pallas_call(guess_kernel, out_shape=(jax.ShapeDtypeStruct((BLK, 2 * S,...  3.86 us

profile of v5, /device:TPU:0, one launch (start us, length us, event | category | flops | bytes accessed | tf_op | source)
XLA Modules:
  0.0 82.1 jit_solution(9542857900597771801)
XLA Ops:
  0.6 77.5 %shard_map.77 = (f32[256,128]{1,0:T(8,128)S(1)}, f32[24,400]{1,0:T(8,128)S(1)}, bf16[16,128,3072]{2,1,0:T(8,128)(2,1)S(1)}) custom-call(bf16[16,128,3072]{2,1,0:T(8,128)(2,1)} %basis.1, bf16[16,24,3072]{2,1,0:T(8,128)(2,1)} %sources.1, bf16[256,3200]{1,0:T(8,128)(2,1)} %coeffs_in.1, s32[1,256]{1,0:T(1,128)} %bitcast.6, s32[1,256]{1,0:T(1,128)} %bitcast.4, ...), custom_call_target="tpu_custom_call" | custom-call | tf_op jit(solution)/shard_map/pallas_call | solution.py:638
  78.1 3.9 %shard_map.78 = (f32[16,24,3072]{2,1,0:T(8,128)}, f32[24,400]{1,0:T(8,128)}) custom-call(f32[256,128]{1,0:T(8,128)S(1)} %get-tuple-element.7.g_in, f32[24,400]{1,0:T(8,128)S(1)} %get-tuple-element.8.corr_in, bf16[16,128,3072]{2,1,0:T(8,128)(2,1)S(1)} %get-tuple-element.9.bbuf), custom_call_target="tpu_custom_call" | custom-call | tf_op jit(solution)/shard_map/pallas_call | solution.py:705
